TPU v7x, 32 devices: a whole 2x2x4 slice. The times are simulated.
32 devices in a mesh: dp: 4 (over x, core), ctx: 8 (over z, y).
Axes of the slice: x: 2, y: 2, z: 4, core: 2. Of those that a mesh axis runs over, the one named last changes fastest.
Arguments:
- hidden_in: bfloat16 [4096, 1024], P(('dp', 'ctx')), may hold values from -6 to 6
- document_index: int32 [4, 1024], P('dp', 'ctx'), may hold values from 0 to 2, never falling along the last dimension, each value on 1 to 768 neighbouring positions
- out_grad: bfloat16 [4096, 1024], P(('dp', 'ctx')), may hold values from -6 to 6
- qkv_weight: bfloat16 [2, 1024, 3072], P(None, ('dp', 'ctx')), may hold values from -0.1875 to 0.1875
- value_bias: bfloat16 [2, 1024], P(None, ('dp', 'ctx')), may hold values from -0.119628906 to 0.119628906
- attention_output_weight: bfloat16 [2, 1024, 1024], P(None, ('dp', 'ctx')), may hold values from -4 to 4
- ffn_in_weight: bfloat16 [2, 1024, 4096], P(None, ('dp', 'ctx')), may hold values from -0.1875 to 0.1875
- ffn_out_weight: bfloat16 [2, 4096, 1024], P(None, ('dp', 'ctx')), may hold values from -0.09375 to 0.09375
- biases: bfloat16 [2, 9216], P(None, ('dp', 'ctx')), may hold values from -1.796875 to 1.796875
- norm_gains: bfloat16 [2, 2048], P(None, ('dp', 'ctx')), may hold values from 0.25 to 1.75
Outputs:
- out: bfloat16 [4096, 1024], P(('dp', 'ctx'))
- input_grad: float32 [4096, 1024], P(('dp', 'ctx'))
- qkv_grad: float32 [2, 1024, 3072], P(None, ('dp', 'ctx'))
- value_bias_grad: float32 [2, 1024], P(None, ('dp', 'ctx'))
- attn_out_grad: float32 [2, 1024, 1024], P(None, ('dp', 'ctx'))
- ffn_in_grad: float32 [2, 1024, 4096], P(None, ('dp', 'ctx'))
- ffn_out_grad: float32 [2, 4096, 1024], P(None, ('dp', 'ctx'))
- bias_grad: float32 [2, 9216], P(None, ('dp', 'ctx'))
- gain_grad: float32 [2, 2048], P(None, ('dp', 'ctx'))
Inputs may be any that keep to these rules, and one draw needn't show every extreme that they name: `document_index`: within each packed row the numbers never fall; every document holds 1 to 768 tokens, and one holds exactly 768.
All inputs are finite; a program needn't handle non-finite values.
Results may differ from a plain program's by a relative error of at most 0.03.
Values may be sent and summed in bfloat16 or wider, within the bound.
A program may use at most 256 MiB of HBM per device.

v0:
```python
import jax
import jax.numpy as jnp
from jax import lax
from jax.sharding import PartitionSpec as P

ATTENTION_HEADS = 16


EPS = 1e-12
NEGATIVE = -1e30


def norm_rows(resid, gain, shift):
    mean = jnp.mean(resid, axis=-1, keepdims=True)
    centered = resid - mean
    variance = jnp.mean(centered * centered, axis=-1, keepdims=True)
    return centered * lax.rsqrt(variance + EPS) * gain + shift


def exact_gelu(value):
    return jax.nn.gelu(value, approximate=False)


def cross(left, right_operand):
    return lax.dot_general(
        left, right_operand, (((0,), (0,)), ((), ())), preferred_element_type=jnp.float32
    )


def back_product(upstream, weight):
    return lax.dot_general(
        upstream, weight, (((1,), (1,)), ((), ())), preferred_element_type=jnp.float32
    )


def by_blocks(step_fn, carry, pieces, token_block):
    count = pieces[0].shape[0]

    def turn(index, state):
        offset = index * token_block
        parts = tuple((lax.dynamic_slice_in_dim(item, offset, token_block, 0) for item in pieces))
        return step_fn(state, parts, offset)

    return lax.fori_loop(0, count // token_block, turn, carry)


def unpack(fetched, width, inner):
    w_qkv, w_out, w_in, w_ffo, value_vec, bias_all, gains = fetched
    value_vec = value_vec.astype(jnp.float32)
    bias_all = bias_all.astype(jnp.float32)
    gains = gains.astype(jnp.float32)
    query_bias = bias_all[0:width]
    out_bias = bias_all[width : 2 * width]
    inner_bias = bias_all[2 * width : 2 * width + inner]
    ffn_bias = bias_all[2 * width + inner : 3 * width + inner]
    shift_one = bias_all[3 * width + inner : 4 * width + inner]
    shift_two = bias_all[4 * width + inner : 5 * width + inner]
    return (
        w_qkv,
        w_out,
        w_in,
        w_ffo,
        value_vec,
        query_bias,
        out_bias,
        inner_bias,
        ffn_bias,
        shift_one,
        shift_two,
        gains[0:width],
        gains[width : 2 * width],
    )


def masked_scores(query_heads, key_piece, seg_own, segment_row, start, scale):
    count = key_piece.shape[0]
    heads = query_heads.shape[1]
    split_key_heads = key_piece.reshape(count, heads, query_heads.shape[2])
    seg_keys = lax.dynamic_slice_in_dim(segment_row, start, count, 0)
    mask = (seg_own[:, None] == seg_keys[None, :])[None]
    raw = (
        jnp.einsum("qhd,khd->hqk", query_heads, split_key_heads, preferred_element_type=jnp.float32)
        * scale
    )
    return (jnp.where(mask, raw, NEGATIVE), mask, split_key_heads)


def body(
    hidden_in,
    document_index,
    out_grad,
    qkv_weight,
    value_bias,
    attention_output_weight,
    ffn_in_weight,
    ffn_out_weight,
    biases,
    norm_gains,
):
    layers = qkv_weight.shape[0]
    width = qkv_weight.shape[2] // 3
    inner = ffn_in_weight.shape[2]
    heads = ATTENTION_HEADS
    head_width = width // heads
    scale = head_width ** (-0.5)
    rows = hidden_in.shape[0]
    seg_own = document_index[0]
    segment_row = lax.all_gather(document_index, "ctx", axis=1, tiled=True)[0]
    row_len = segment_row.shape[0]
    state = hidden_in.astype(jnp.float32)
    saved = []
    for layer in range(layers):
        fetched = (
            lax.all_gather(qkv_weight[layer], ("dp", "ctx"), axis=0, tiled=True),
            lax.all_gather(attention_output_weight[layer], ("dp", "ctx"), axis=0, tiled=True),
            lax.all_gather(ffn_in_weight[layer], ("dp", "ctx"), axis=0, tiled=True),
            lax.all_gather(ffn_out_weight[layer], ("dp", "ctx"), axis=0, tiled=True),
            lax.all_gather(value_bias[layer], ("dp", "ctx"), axis=0, tiled=True),
            lax.all_gather(biases[layer], ("dp", "ctx"), axis=0, tiled=True),
            lax.all_gather(norm_gains[layer], ("dp", "ctx"), axis=0, tiled=True),
        )
        (
            w_qkv,
            w_out,
            w_in,
            w_ffo,
            value_vec,
            query_bias,
            out_bias,
            inner_bias,
            ffn_bias,
            shift_one,
            shift_two,
            gain_one,
            gain_two,
        ) = unpack(fetched, width, inner)
        state_low = state.astype(jnp.bfloat16)
        qkv_bias = jnp.concatenate([query_bias, jnp.zeros_like(query_bias), value_vec])
        qkv_low = (jnp.dot(state_low, w_qkv, preferred_element_type=jnp.float32) + qkv_bias).astype(
            jnp.bfloat16
        )
        query_heads = qkv_low[:, 0:width].reshape(rows, heads, head_width)
        key_low = qkv_low[:, width : 2 * width]
        value_low = qkv_low[:, 2 * width : 3 * width]

        def stats_step(carry, parts, start):
            top, total = carry
            raw, mask, split_key_heads = masked_scores(
                query_heads, parts[0], seg_own, segment_row, start, scale
            )
            new_top = jnp.maximum(top, jnp.max(raw, axis=-1))
            weights = jnp.where(mask, jnp.exp(raw - new_top[:, :, None]), 0.0)
            return (new_top, total * jnp.exp(top - new_top) + jnp.sum(weights, axis=-1))

        stats_init = (
            jnp.full((heads, rows), NEGATIVE, jnp.float32),
            jnp.zeros((heads, rows), jnp.float32),
        )
        held_pair = None
        top, total = by_blocks(
            stats_step, stats_init, (lax.all_gather(key_low, "ctx", axis=0, tiled=True),), rows
        )
        log_total = top + jnp.log(total)

        def value_step(carry, parts, start):
            context_acc, exact_acc = carry
            raw, mask, split_key_heads = masked_scores(
                query_heads, parts[0], seg_own, segment_row, start, scale
            )
            split_value_heads = parts[1].reshape(parts[1].shape[0], heads, head_width)
            probs = jnp.where(mask, jnp.exp(raw - log_total[:, :, None]), 0.0)
            probs_low = probs.astype(jnp.bfloat16)
            residue_low = (probs - probs_low.astype(jnp.float32)).astype(jnp.bfloat16)
            part_low = jnp.einsum(
                "hqk,khd->qhd", probs_low, split_value_heads, preferred_element_type=jnp.float32
            )
            part_fix = jnp.einsum(
                "hqk,khd->qhd", residue_low, split_value_heads, preferred_element_type=jnp.float32
            )
            return (context_acc + part_low, exact_acc + part_fix)

        value_init = (
            jnp.zeros((rows, heads, head_width), jnp.float32),
            jnp.zeros((rows, heads, head_width), jnp.float32),
        )
        context, correction = by_blocks(
            value_step,
            value_init,
            (
                lax.all_gather(key_low, "ctx", axis=0, tiled=True),
                lax.all_gather(value_low, "ctx", axis=0, tiled=True),
            ),
            rows,
        )
        context_exact = (context + correction).reshape(rows, width)
        context = context.reshape(rows, width)
        context_low = context.astype(jnp.bfloat16)
        resid_one = (
            state + jnp.dot(context_low, w_out, preferred_element_type=jnp.float32) + out_bias
        )
        normed = norm_rows(resid_one, gain_one, shift_one)
        normed_low = normed.astype(jnp.bfloat16)
        pre = jnp.dot(normed_low, w_in, preferred_element_type=jnp.float32) + inner_bias
        inner_low = exact_gelu(pre).astype(jnp.bfloat16)
        resid_two = (
            normed + jnp.dot(inner_low, w_ffo, preferred_element_type=jnp.float32) + ffn_bias
        )
        saved.append(
            (
                fetched,
                state_low,
                qkv_low,
                log_total,
                context_exact,
                context_low,
                resid_one,
                normed_low,
                pre,
                inner_low,
                resid_two,
                held_pair,
            )
        )
        state = norm_rows(resid_two, gain_two, shift_two)
    upstream = out_grad.astype(jnp.float32)
    per_layer = []
    for layer in reversed(range(layers)):
        (
            fetched,
            state_low,
            qkv_low,
            log_total,
            context_exact,
            context_low,
            resid_one,
            normed_low,
            pre,
            inner_low,
            resid_two,
            held_pair,
        ) = saved[layer]
        weights_now = (
            lax.all_gather(qkv_weight[layer], ("dp", "ctx"), axis=0, tiled=True),
            lax.all_gather(attention_output_weight[layer], ("dp", "ctx"), axis=0, tiled=True),
            lax.all_gather(ffn_in_weight[layer], ("dp", "ctx"), axis=0, tiled=True),
            lax.all_gather(ffn_out_weight[layer], ("dp", "ctx"), axis=0, tiled=True),
            lax.all_gather(value_bias[layer], ("dp", "ctx"), axis=0, tiled=True),
            lax.all_gather(biases[layer], ("dp", "ctx"), axis=0, tiled=True),
            lax.all_gather(norm_gains[layer], ("dp", "ctx"), axis=0, tiled=True),
        )
        (
            w_qkv,
            w_out,
            w_in,
            w_ffo,
            value_vec,
            query_bias,
            out_bias,
            inner_bias,
            ffn_bias,
            shift_one,
            shift_two,
            gain_one,
            gain_two,
        ) = unpack(weights_now, width, inner)
        query_low = qkv_low[:, 0:width]
        query_heads = query_low.reshape(rows, heads, head_width)
        key_low = qkv_low[:, width : 2 * width]
        value_low = qkv_low[:, 2 * width : 3 * width]
        unused_two, pull_two = jax.vjp(norm_rows, resid_two, gain_two, shift_two)
        back_two, back_gain_two, back_shift_two = pull_two(upstream)
        back_second = back_two.astype(jnp.bfloat16)
        grad_second = cross(inner_low, back_second)
        back_inner = back_product(back_second, w_ffo)
        unused_pre, pull_gelu = jax.vjp(exact_gelu, pre)
        back_pre = pull_gelu(back_inner)[0].astype(jnp.bfloat16)
        grad_first = cross(normed_low, back_pre)
        back_normed = back_two + back_product(back_pre, w_in)
        normed_again, pull_one = jax.vjp(norm_rows, resid_one, gain_one, shift_one)
        back_one, back_gain_one, back_shift_one = pull_one(back_normed)
        back_branch = back_one.astype(jnp.bfloat16)
        grad_out_proj = cross(context_low, back_branch)
        back_context = back_product(back_branch, w_out).astype(jnp.bfloat16)
        context_heads_back = back_context.reshape(rows, heads, head_width)
        delta = jnp.sum(
            (back_context.astype(jnp.float32) * context_exact).reshape(rows, heads, head_width),
            axis=-1,
        ).T

        def grad_step(carry, parts, start):
            query_sum, key_sums, value_sums = carry
            count = parts[0].shape[0]
            raw, mask, split_key_heads = masked_scores(
                query_heads, parts[0], seg_own, segment_row, start, scale
            )
            split_value_heads = parts[1].reshape(count, heads, head_width)
            probs = jnp.where(mask, jnp.exp(raw - log_total[:, :, None]), 0.0)
            back_probs = jnp.einsum(
                "qhd,khd->hqk",
                context_heads_back,
                split_value_heads,
                preferred_element_type=jnp.float32,
            )
            back_scores = (probs * (back_probs - delta[:, :, None])).astype(jnp.bfloat16)
            query_part = (
                jnp.einsum(
                    "hqk,khd->qhd", back_scores, split_key_heads, preferred_element_type=jnp.float32
                )
                * scale
            )
            key_part = (
                jnp.einsum(
                    "hqk,qhd->khd", back_scores, query_heads, preferred_element_type=jnp.float32
                ).reshape(count, width)
                * scale
            )
            value_part = jnp.einsum(
                "hqk,qhd->khd",
                probs.astype(jnp.bfloat16),
                context_heads_back,
                preferred_element_type=jnp.float32,
            ).reshape(count, width)
            key_sums = lax.dynamic_update_slice_in_dim(
                key_sums, lax.dynamic_slice_in_dim(key_sums, start, count, 0) + key_part, start, 0
            )
            value_sums = lax.dynamic_update_slice_in_dim(
                value_sums,
                lax.dynamic_slice_in_dim(value_sums, start, count, 0) + value_part,
                start,
                0,
            )
            return (query_sum + query_part, key_sums, value_sums)

        query_init = jnp.zeros((rows, heads, head_width), jnp.float32)
        grad_init = (
            query_init,
            jnp.zeros((row_len, width), jnp.float32),
            jnp.zeros((row_len, width), jnp.float32),
        )
        folded = by_blocks(
            grad_step,
            grad_init,
            (
                lax.all_gather(key_low, "ctx", axis=0, tiled=True),
                lax.all_gather(value_low, "ctx", axis=0, tiled=True),
            ),
            rows,
        )
        query_sum, key_sums, value_sums = folded
        key_own, value_own = (
            lax.psum_scatter(
                key_sums.astype(jnp.bfloat16), "ctx", scatter_dimension=0, tiled=True
            ).astype(jnp.float32),
            lax.psum_scatter(
                value_sums.astype(jnp.bfloat16), "ctx", scatter_dimension=0, tiled=True
            ).astype(jnp.float32),
        )
        back_qkv = jnp.concatenate(
            [query_sum.reshape(rows, width), key_own, value_own], axis=1
        ).astype(jnp.bfloat16)
        grad_qkv = cross(state_low, back_qkv)
        back_qkv_float = back_qkv.astype(jnp.float32)
        grad_value_bias = jnp.sum(back_qkv_float[:, 2 * width : 3 * width], axis=0)
        grad_bias = jnp.concatenate(
            [
                jnp.sum(back_qkv_float[:, 0:width], axis=0),
                jnp.sum(back_branch.astype(jnp.float32), axis=0),
                jnp.sum(back_pre.astype(jnp.float32), axis=0),
                jnp.sum(back_second.astype(jnp.float32), axis=0),
                back_shift_one,
                back_shift_two,
            ]
        )
        grad_gain = jnp.concatenate([back_gain_one, back_gain_two])
        upstream = back_one + back_product(back_qkv, w_qkv)
        shards = (
            lax.psum_scatter(grad_qkv, ("dp", "ctx"), scatter_dimension=0, tiled=True),
            lax.psum_scatter(grad_value_bias, ("dp", "ctx"), scatter_dimension=0, tiled=True),
            lax.psum_scatter(grad_out_proj, ("dp", "ctx"), scatter_dimension=0, tiled=True),
            lax.psum_scatter(grad_first, ("dp", "ctx"), scatter_dimension=0, tiled=True),
            lax.psum_scatter(grad_second, ("dp", "ctx"), scatter_dimension=0, tiled=True),
            lax.psum_scatter(grad_bias, ("dp", "ctx"), scatter_dimension=0, tiled=True),
            lax.psum_scatter(grad_gain, ("dp", "ctx"), scatter_dimension=0, tiled=True),
        )
        per_layer.append(shards)
    ordered = per_layer[::-1]
    stacked = tuple((jnp.stack([item[member] for item in ordered]) for member in range(7)))
    return (
        state.astype(jnp.bfloat16),
        upstream,
        stacked[0],
        stacked[1],
        stacked[2],
        stacked[3],
        stacked[4],
        stacked[5],
        stacked[6],
    )


def solution(mesh):
    return jax.shard_map(
        body,
        mesh=mesh,
        in_specs=(
            P(("dp", "ctx"), None),
            P("dp", "ctx"),
            P(("dp", "ctx"), None),
            P(None, ("dp", "ctx"), None),
            P(None, ("dp", "ctx")),
            P(None, ("dp", "ctx"), None),
            P(None, ("dp", "ctx"), None),
            P(None, ("dp", "ctx"), None),
            P(None, ("dp", "ctx")),
            P(None, ("dp", "ctx")),
        ),
        out_specs=(
            P(("dp", "ctx"), None),
            P(("dp", "ctx"), None),
            P(None, ("dp", "ctx"), None),
            P(None, ("dp", "ctx")),
            P(None, ("dp", "ctx"), None),
            P(None, ("dp", "ctx"), None),
            P(None, ("dp", "ctx"), None),
            P(None, ("dp", "ctx")),
            P(None, ("dp", "ctx")),
        ),
        check_vma=False,
    )
```

profile of v0, /device:TPU:0, one launch (start us, length us, event | category | flops | bytes accessed | tf_op | source)
XLA Modules:
  0.0 3441.1 jit_solution(7078647340704805282)
XLA Ops:
  12.7 43.0 %all-reduce.13 = (bf16[9216]{0:T(1024)(128)(2,1)S(1)}, bf16[1024]{0:T(1024)(128)(2,1)S(1)}, bf16[9216]{0:T(1024)(128)(2,1)S(1)}, bf16[1024]{0:T(1024)(128)(2,1)S...) all-reduce(bf16[9216]{0:T(1024)(128)(2,1)S(1)} %dynamic-update-slic, ...), channel_id=10, replica_groups=mesh['dp'=4,'ctx'=8] {'dp','ctx'}, use_global_device_ids=true, to_apply=%add.3 | all-reduce | flops 24576 | bytes 98304
  55.8 28.1 all-gather.35.cloned.1.call-done
  83.9 3.9 fusion.87
  92.8 19.1 all_gather.77
  112.1 24.5 all-gather.29.cloned.1.call-done
  136.6 3.9 copy.94
  140.6 14.4 while.100
  155.0 32.2 all-gather.27.cloned.1.call-done
  187.1 3.9 copy.93
  191.1 18.5 while.101
  210.5 34.5 %all-gather.37.cloned.1.call-done = bf16[1,1024,1024]{2,1,0:T(8,128)(2,1)} async-done(((bf16[1,32,1024]{2,1,0:T(8,128)(2,1)}), bf16[1,1024,1024]{2,1,0:T(8,128)(2,1)}) %all-gather.37.cloned.1.call-update) | async-done | bytes 2097168 | tf_op jit(solution)/shard_map/all_gather | solution.py:115
  247.4 77.2 %all-gather.39.cloned.1.call-done = bf16[1,1024,4096]{2,1,0:T(8,128)(2,1)} async-done(((bf16[1,32,4096]{2,1,0:T(8,128)(2,1)}), bf16[1,1024,4096]{2,1,0:T(8,128)(2,1)}) %all-gather.39.cloned.1.call-update) | async-done | bytes 8388624 | tf_op jit(solution)/shard_map/all_gather | solution.py:116
  324.6 9.1 multiply_convert_fusion.1
  333.7 70.3 %all-gather.41.cloned.1.call-done = bf16[1,4096,1024]{2,1,0:T(8,128)(2,1)} async-done(((bf16[1,128,1024]{2,1,0:T(8,128)(2,1)}), bf16[1,4096,1024]{2,1,0:T(8,128)(2,1)}) %all-gather.41.cloned.1.call-update) | async-done | bytes 8388624 | tf_op jit(solution)/shard_map/all_gather | solution.py:117
  404.1 4.8 fusion.199
  409.1 66.0 %all-gather.43.cloned.1.call-done = bf16[1,1024,3072]{2,1,0:T(8,128)(2,1)} async-done(((bf16[1,32,3072]{2,1,0:T(8,128)(2,1)}), bf16[1,1024,3072]{2,1,0:T(8,128)(2,1)}) %all-gather.43.cloned.1.call-update) | async-done | bytes 6291472 | tf_op jit(solution)/shard_map/all_gather | solution.py:114
  475.1 3.8 fusion.84
  483.0 44.8 %all-gather.33.cloned.1.call-done = bf16[1024,1024]{1,0:T(8,128)(2,1)} async-done(((bf16[128,1024]{1,0:T(8,128)(2,1)}), bf16[1024,1024]{1,0:T(8,128)(2,1)}) %all-gather.33.cloned.1.call-update) | async-done | bytes 2097168 | tf_op jit(solution)/shard_map/all_gather | solution.py:190
  527.8 4.0 copy.98
  531.7 14.4 while.102
  546.1 32.3 all-gather.31.cloned.1.call-done
  578.4 4.0 copy.97
  582.4 18.5 while.103
  601.8 34.5 %all-gather.45.cloned.1.call-done = bf16[1,1024,1024]{2,1,0:T(8,128)(2,1)} async-done(((bf16[1,32,1024]{2,1,0:T(8,128)(2,1)}), bf16[1,1024,1024]{2,1,0:T(8,128)(2,1)}) %all-gather.45.cloned.1.call-update) | async-done | bytes 2097168 | tf_op jit(solution)/shard_map/all_gather | solution.py:115
  638.7 77.3 %all-gather.47.cloned.1.call-done = bf16[1,1024,4096]{2,1,0:T(8,128)(2,1)} async-done(((bf16[1,32,4096]{2,1,0:T(8,128)(2,1)}), bf16[1,1024,4096]{2,1,0:T(8,128)(2,1)}) %all-gather.47.cloned.1.call-update) | async-done | bytes 8388624 | tf_op jit(solution)/shard_map/all_gather | solution.py:116
  716.1 9.1 multiply_convert_fusion
  725.2 70.4 %all-gather.49.cloned.1.call-done = bf16[1,4096,1024]{2,1,0:T(8,128)(2,1)} async-done(((bf16[1,128,1024]{2,1,0:T(8,128)(2,1)}), bf16[1,4096,1024]{2,1,0:T(8,128)(2,1)}) %all-gather.49.cloned.1.call-update) | async-done | bytes 8388624 | tf_op jit(solution)/shard_map/all_gather | solution.py:117
  795.5 4.9 fusion.201
  802.3 8.0 convert_reduce_fusion
  823.9 52.3 %while.104 = (s32[]{:T(128)}, f32[128,16,64]{0,2,1:T(8,128)S(1)}, f32[1024,1024]{0,1:T(8,128)}, f32[1024,1024]{0,1:T(8,128)}, bf16[1024,1024]{0,1:T(8,128)(2,1)}...) while((s32[]{:T(128)}, f32[128,16,64]{0,2,1:T(8,128)S(1)}, ...), condition=%wide.region_26.27_spmd.clone, body=%wide.region_25.26_spmd.clone.sunk | while | flops 170672128 | bytes 12896477 | solution.py:44
  876.3 3.9 convert_element_type.230
  880.1 3.9 copy.123
  884.1 3.9 convert_element_type.231
  888.0 4.0 copy.125
  893.3 57.3 %reduce-scatter.37.cloned.1.call-done = bf16[128,1024]{1,0:T(8,128)(2,1)} async-done(((bf16[1024,1024]{1,0:T(8,128)(2,1)}), bf16[128,1024]{1,0:T(8,128)(2,1)}) %reduce-scatter.37.cloned.1.call-update) | async-done | bytes 262160
  951.8 69.1 %reduce-scatter.39.cloned.1.call-done = bf16[128,1024]{1,0:T(8,128)(2,1)} async-done(((bf16[1024,1024]{1,0:T(8,128)(2,1)}), bf16[128,1024]{1,0:T(8,128)(2,1)}) %reduce-scatter.39.cloned.1.call-update) | async-done | bytes 262160
  1022.0 5.9 multiply_reduce_fusion.1
  1029.6 9.8 convert_reduce_fusion.1
  1050.7 57.7 %while.105 = (s32[]{:T(128)}, f32[128,16,64]{0,2,1:T(8,128)S(1)}, f32[1024,1024]{0,1:T(8,128)}, f32[1024,1024]{0,1:T(8,128)}, bf16[1024,1024]{0,1:T(8,128)(2,1)}...) while((s32[]{:T(128)}, f32[128,16,64]{0,2,1:T(8,128)S(1)}, ...), condition=%wide.region_35.36_spmd.clone, body=%wide.region_34.35_spmd.clone.sunk | while | flops 170672128 | bytes 12896477 | solution.py:44
  1108.4 3.9 convert_element_type.237
  1112.2 3.9 copy.127
  1116.3 3.9 convert_element_type.238
  1120.1 4.0 copy.129
  1126.9 56.1 %reduce-scatter.41.cloned.1.call-done = bf16[128,1024]{1,0:T(8,128)(2,1)} async-done(((bf16[1024,1024]{1,0:T(8,128)(2,1)}), bf16[128,1024]{1,0:T(8,128)(2,1)}) %reduce-scatter.41.cloned.1.call-update) | async-done | bytes 262160
  1184.2 68.9 %reduce-scatter.43.cloned.1.call-done = bf16[128,1024]{1,0:T(8,128)(2,1)} async-done(((bf16[1024,1024]{1,0:T(8,128)(2,1)}), bf16[128,1024]{1,0:T(8,128)(2,1)}) %reduce-scatter.43.cloned.1.call-update) | async-done | bytes 262160
  1256.2 3.6 fusion.203
  1260.8 3.6 fusion.202
  1265.1 6.5 fusion.171
  1272.5 6.3 convolution_bitcast_fusion.4
  1278.8 12.7 copy.131
  1292.7 8.2 fusion.172
  1302.1 8.2 fusion.177
  1311.6 8.1 fusion.205
  1321.0 8.1 fusion.204
  1330.2 5.8 fusion.144
  1336.0 46.1 %all-reduce.16.cloned.1.call-done = (f32[1024]{0:T(1024)}, f32[1024]{0:T(1024)}, f32[9216]{0:T(1024)}, f32[9216]{0:T(1024)}, f32[2048]{0:T(1024)}, /*index=5*/f32[2048]{0:T(1024)}) async-done(((f32[1024]{0:T(1024)}, f32[1024]{0:T(1024)}, f32[9216]{0:T(1024)}, f32[9216]{0:T(1024)}, f32[2048]{0:T(1024)}, /*index=5*/f32[2048]{0:T(1024)}), (f32[1024]{0:T(1024)}, f32[1024]{0:T(1024)}, f32[9216]{0:T(1024)}, ...) | async-done | bytes 98320
  1387.0 142.0 %reduce-scatter.27.cloned.1.call-done = f32[32,1024]{1,0:T(8,128)} async-done(((f32[1024,1024]{1,0:T(8,128)}), f32[32,1024]{1,0:T(8,128)}) %reduce-scatter.27.cloned.1.call-update) | async-done | bytes 131088 | tf_op jit(solution)/shard_map/reduce_scatter | solution.py:379
  1529.0 144.2 %reduce-scatter.25.cloned.1.call-done = f32[32,1024]{1,0:T(8,128)} async-done(((f32[1024,1024]{1,0:T(8,128)}), f32[32,1024]{1,0:T(8,128)}) %reduce-scatter.25.cloned.1.call-update) | async-done | bytes 131088 | tf_op jit(solution)/shard_map/reduce_scatter | solution.py:379
  1674.8 157.3 %reduce-scatter.47.cloned.1.call-done = f32[32,3072]{1,0:T(8,128)} async-done(((f32[1024,3072]{1,0:T(8,128)}), f32[32,3072]{1,0:T(8,128)}) %reduce-scatter.47.cloned.1.call-update) | async-done | bytes 393232
  1834.0 159.7 %reduce-scatter.45.cloned.1.call-done = f32[32,3072]{1,0:T(8,128)} async-done(((f32[1024,3072]{1,0:T(8,128)}), f32[32,3072]{1,0:T(8,128)}) %reduce-scatter.45.cloned.1.call-update) | async-done | bytes 393232
  1996.5 356.7 %reduce-scatter.31.cloned.1.call-done = f32[32,4096]{1,0:T(8,128)} async-done(((f32[1024,4096]{1,0:T(8,128)}), f32[32,4096]{1,0:T(8,128)}) %reduce-scatter.31.cloned.1.call-update) | async-done | bytes 524304 | tf_op jit(solution)/shard_map/reduce_scatter | solution.py:380
  2353.2 359.7 %reduce-scatter.29.cloned.1.call-done = f32[32,4096]{1,0:T(8,128)} async-done(((f32[1024,4096]{1,0:T(8,128)}), f32[32,4096]{1,0:T(8,128)}) %reduce-scatter.29.cloned.1.call-update) | async-done | bytes 524304 | tf_op jit(solution)/shard_map/reduce_scatter | solution.py:380
  2715.1 357.3 %reduce-scatter.35.cloned.1.call-done = f32[128,1024]{1,0:T(8,128)} async-done(((f32[4096,1024]{1,0:T(8,128)}), f32[128,1024]{1,0:T(8,128)}) %reduce-scatter.35.cloned.1.call-update) | async-done | bytes 524304 | tf_op jit(solution)/shard_map/reduce_scatter | solution.py:381
  3072.4 359.7 %reduce-scatter.33.cloned.1.call-done = f32[128,1024]{1,0:T(8,128)} async-done(((f32[4096,1024]{1,0:T(8,128)}), f32[128,1024]{1,0:T(8,128)}) %reduce-scatter.33.cloned.1.call-update) | async-done | bytes 524304 | tf_op jit(solution)/shard_map/reduce_scatter | solution.py:381
  (722 shorter events, 256.9 us)
Async XLA Ops:
  7.2 76.7 %all-gather.35.cloned.1.call-start = ((), (), s32[]{:S(2)}) async-start(), calls=%async_computation.22 | async-start | bytes 6488064 | tf_op jit(solution)/shard_map/all_gather | solution.py:114
  9.0 127.6 %all-gather.29.cloned.1.call-start = ((), (), s32[]{:S(2)}) async-start(), calls=%async_computation.13 | async-start | bytes 2359296 | tf_op jit(solution)/shard_map/all_gather | solution.py:190
  55.7 348.3 %copy-start.42 = (f32[1,1024]{1,0:T(1,128)}, f32[1,1024]{1,0:T(1,128)S(1)}, u32[]{:S(2)}) copy-start(f32[1,1024]{1,0:T(1,128)S(1)} %get-tuple-element.1553) | copy-start | bytes 12292
  87.8 3.3 copy-start.40
  88.7 4.2 copy-start.41
  88.7 98.4 %all-gather.27.cloned.1.call-start = ((), (), s32[]{:S(2)}) async-start(), calls=%async_computation.12 | async-start | bytes 2359296 | tf_op jit(solution)/shard_map/all_gather | solution.py:191
  89.4 155.6 %all-gather.37.cloned.1.call-start = ((), (), s32[]{:S(2)}) async-start(), calls=%async_computation.23 | async-start | bytes 2162688 | tf_op jit(solution)/shard_map/all_gather | solution.py:115
  90.2 234.5 %all-gather.39.cloned.1.call-start = ((), (), s32[]{:S(2)}) async-start(), calls=%async_computation.24 | async-start | bytes 8650752 | tf_op jit(solution)/shard_map/all_gather | solution.py:116
  91.1 313.0 %all-gather.41.cloned.1.call-start = ((), (), s32[]{:S(2)}) async-start(), calls=%async_computation.25 | async-start | bytes 8650752 | tf_op jit(solution)/shard_map/all_gather | solution.py:117
  92.0 383.1 %all-gather.43.cloned.1.call-start = ((), (), s32[]{:S(2)}) async-start(), calls=%async_computation.26 | async-start | bytes 6488064 | tf_op jit(solution)/shard_map/all_gather | solution.py:114
  92.7 435.0 %all-gather.33.cloned.1.call-start = ((), (), s32[]{:S(2)}) async-start(), calls=%async_computation.15 | async-start | bytes 2359296 | tf_op jit(solution)/shard_map/all_gather | solution.py:190
  191.1 54.0 %copy-start.14 = (bf16[128,1024]{1,0:T(8,128)(2,1)S(1)}, bf16[128,1024]{1,0:T(8,128)(2,1)}, u32[]{:S(2)}) copy-start(bf16[128,1024]{1,0:T(8,128)(2,1)} %param.22) | copy-start | bytes 786436
  209.6 35.4 %copy-start.54 = (f32[16,128]{1,0:T(8,128)}, f32[16,128]{1,0:T(8,128)S(1)}, u32[]{:S(2)}) copy-start(f32[16,128]{1,0:T(8,128)S(1)} %get-tuple-element.2329) | copy-start | bytes 24580
  210.5 123.2 %copy-start.28 = (bf16[128,16,64]{0,2,1:T(8,128)(2,1)}, bf16[128,16,64]{0,2,1:T(8,128)(2,1)S(1)}, u32[]{:S(2)}) copy-start(bf16[128,16,64]{0,2,1:T(8,128)(2,1)S(1)} %get-tuple-element.1535) | copy-start | bytes 786436
  247.4 86.3 %copy-start.61 = (f32[128]{0:T(128)}, f32[128]{0:T(128)S(1)}, u32[]{:S(2)}) copy-start(f32[128]{0:T(128)S(1)} %multiply_reduce_fusion.9) | copy-start | bytes 1540
  247.4 156.6 %copy-start.47 = (f32[128]{0:T(128)}, f32[128]{0:T(128)S(1)}, u32[]{:S(2)}) copy-start(f32[128]{0:T(128)S(1)} %fusion.165) | copy-start | bytes 1540
  333.7 75.1 %copy-start.5 = (bf16[128,4096]{1,0:T(8,128)(2,1)}, bf16[128,4096]{1,0:T(8,128)(2,1)S(1)}, u32[]{:S(2)}) copy-start(bf16[128,4096]{1,0:T(8,128)(2,1)S(1)} %get-tuple-element.1568) | copy-start | bytes 3145732
  408.9 70.1 %copy-start = (f32[128,1024]{1,0:T(8,128)}, f32[128,1024]{1,0:T(8,128)S(1)}, u32[]{:S(2)}) copy-start(f32[128,1024]{1,0:T(8,128)S(1)} %get-tuple-element.1571) | copy-start | bytes 1572868
  408.9 619.1 %copy-start.52 = (f32[128]{0:T(128)}, f32[128]{0:T(128)S(1)}, u32[]{:S(2)}) copy-start(f32[128]{0:T(128)S(1)} %broadcast_multiply_fusion.2) | copy-start | bytes 1540
  409.1 618.9 %copy-start.56 = (f32[128]{0:T(128)}, f32[128]{0:T(128)S(1)}, u32[]{:S(2)}) copy-start(f32[128]{0:T(128)S(1)} %fusion.166) | copy-start | bytes 1540
  479.8 98.6 %all-gather.31.cloned.1.call-start = ((), (), s32[]{:S(2)}) async-start(), calls=%async_computation.14 | async-start | bytes 2359296 | tf_op jit(solution)/shard_map/all_gather | solution.py:191
  480.6 155.8 %all-gather.45.cloned.1.call-start = ((), (), s32[]{:S(2)}) async-start(), calls=%async_computation.27 | async-start | bytes 2162688 | tf_op jit(solution)/shard_map/all_gather | solution.py:115
  481.2 234.9 %all-gather.47.cloned.1.call-start = ((), (), s32[]{:S(2)}) async-start(), calls=%async_computation.28 | async-start | bytes 8650752 | tf_op jit(solution)/shard_map/all_gather | solution.py:116
  481.9 313.6 %all-gather.49.cloned.1.call-start = ((), (), s32[]{:S(2)}) async-start(), calls=%async_computation.29 | async-start | bytes 8650752 | tf_op jit(solution)/shard_map/all_gather | solution.py:117
  482.5 468.2 %reduce-scatter.37.cloned.1.call-start = ((), (), s32[]{:S(2)}) async-start(), calls=%async_computation.30 | async-start | bytes 2359296
  600.9 35.4 %copy-start.1 = (f32[128,1024]{1,0:T(8,128)S(1)}, f32[128,1024]{1,0:T(8,128)}, u32[]{:S(2)}) copy-start(f32[128,1024]{1,0:T(8,128)} %copy-done) | copy-start | bytes 1572868
  601.8 114.3 %copy-start.29 = (bf16[128,16,64]{0,2,1:T(8,128)(2,1)}, bf16[128,16,64]{0,2,1:T(8,128)(2,1)S(1)}, u32[]{:S(2)}) copy-start(bf16[128,16,64]{0,2,1:T(8,128)(2,1)S(1)} %get-tuple-element.1537) | copy-start | bytes 786436
  638.7 174.7 %copy-start.50 = (f32[128]{0:T(128)}, f32[128]{0:T(128)S(1)}, u32[]{:S(2)}) copy-start(f32[128]{0:T(128)S(1)} %fusion.167) | copy-start | bytes 1540
  725.2 75.3 %copy-start.7 = (bf16[128,4096]{1,0:T(8,128)(2,1)}, bf16[128,4096]{1,0:T(8,128)(2,1)S(1)}, u32[]{:S(2)}) copy-start(bf16[128,4096]{1,0:T(8,128)(2,1)S(1)} %get-tuple-element.1574) | copy-start | bytes 3145732
  795.5 6.6 slice-start
  795.5 5.2 copy-start.38
  795.5 6.6 slice-start.1
  801.0 9.3 slice-start.4
  802.1 8.2 copy-start.34
  802.3 8.0 slice-start.5
  810.3 3.1 copy-start.10
  810.4 4.1 copy-start.31
  876.2 3.9 copy-start.58
  884.1 136.7 %reduce-scatter.39.cloned.1.call-start = ((), (), s32[]{:S(2)}) async-start(), calls=%async_computation.31 | async-start | bytes 2359296
  892.0 130.0 %copy-start.2 = (f32[128,1024]{1,0:T(8,128)S(1)}, f32[128,1024]{1,0:T(8,128)}, u32[]{:S(2)}) copy-start(f32[128,1024]{1,0:T(8,128)} %copy-done) | copy-start | bytes 1572868
  892.0 291.0 %reduce-scatter.41.cloned.1.call-start = ((), (), s32[]{:S(2)}) async-start(), calls=%async_computation.32 | async-start | bytes 2359296
  893.3 134.6 %copy-start.16 = (bf16[128,16,64]{0,2,1:T(8,128)(2,1)}, bf16[128,16,64]{0,2,1:T(8,128)(2,1)S(1)}, u32[]{:S(2)}) copy-start(bf16[128,16,64]{0,2,1:T(8,128)(2,1)S(1)} %convert.12) | copy-start | bytes 786436
  951.7 76.2 %copy-start.20 = (bf16[128,1024]{0,1:T(8,128)(2,1)}, bf16[128,1024]{0,1:T(8,128)(2,1)S(1)}, u32[]{:S(2)}) copy-start(bf16[128,1024]{0,1:T(8,128)(2,1)S(1)} %copy.124) | copy-start | bytes 786436
  1021.9 6.0 copy-start.22
  1022.0 17.5 slice-start.2
  1028.4 11.0 copy-start.36
  1029.6 9.8 slice-start.3
  1029.6 9.8 copy-start.48
  1039.4 3.1 copy-start.12
  1039.5 3.1 copy-start.62
  1116.2 136.9 %reduce-scatter.43.cloned.1.call-start = ((), (), s32[]{:S(2)}) async-start(), calls=%async_computation.33 | async-start | bytes 2359296
  1124.1 258.1 %all-reduce.16.cloned.1.call-start = ((), (), s32[]{:S(2)}) async-start(), calls=%async_computation.36 | async-start | bytes 196608
  1125.2 146.4 %copy-start.18 = (bf16[128,16,64]{0,2,1:T(8,128)(2,1)}, bf16[128,16,64]{0,2,1:T(8,128)(2,1)S(1)}, u32[]{:S(2)}) copy-start(bf16[128,16,64]{0,2,1:T(8,128)(2,1)S(1)} %convert.13) | copy-start | bytes 786436
  1126.3 129.0 %copy-start.45 = (f32[9216]{0:T(1024)}, f32[9216]{0:T(1024)S(1)}, u32[]{:S(2)}) copy-start(f32[9216]{0:T(1024)S(1)} %constant_dynamic-update-slice_fusion.5) | copy-start | bytes 110596
  1184.1 71.1 %copy-start.59 = (f32[1024]{0:T(1024)S(1)}, f32[1024]{0:T(1024)}, u32[]{:S(2)}) copy-start(f32[1024]{0:T(1024)} %get-tuple-element.1370) | copy-start | bytes 12292
  1184.2 72.0 %copy-start.25 = (bf16[128,1024]{1,0:T(8,128)(2,1)S(1)}, bf16[128,1024]{1,0:T(8,128)(2,1)}, u32[]{:S(2)}) copy-start(bf16[128,1024]{1,0:T(8,128)(2,1)} %copy-done.24) | copy-start | bytes 786436
  1255.9 273.0 %reduce-scatter.27.cloned.1.call-start = ((), (), s32[]{:S(2)}) async-start(), calls=%async_computation.17 | async-start | bytes 4325376 | tf_op jit(solution)/shard_map/reduce_scatter | solution.py:379
  1259.9 413.3 %reduce-scatter.25.cloned.1.call-start = ((), (), s32[]{:S(2)}) async-start(), calls=%async_computation.16 | async-start | bytes 4325376 | tf_op jit(solution)/shard_map/reduce_scatter | solution.py:379
  1264.4 567.7 %reduce-scatter.47.cloned.1.call-start = ((), (), s32[]{:S(2)}) async-start(), calls=%async_computation.35 | async-start | bytes 12976128
  1271.6 722.1 %reduce-scatter.45.cloned.1.call-start = ((), (), s32[]{:S(2)}) async-start(), calls=%async_computation.34 | async-start | bytes 12976128
  1291.5 1061.7 %reduce-scatter.31.cloned.1.call-start = ((), (), s32[]{:S(2)}) async-start(), calls=%async_computation.19 | async-start | bytes 17301504 | tf_op jit(solution)/shard_map/reduce_scatter | solution.py:380
  1300.9 1412.0 %reduce-scatter.29.cloned.1.call-start = ((), (), s32[]{:S(2)}) async-start(), calls=%async_computation.18 | async-start | bytes 17301504 | tf_op jit(solution)/shard_map/reduce_scatter | solution.py:380
  1310.4 1762.0 %reduce-scatter.35.cloned.1.call-start = ((), (), s32[]{:S(2)}) async-start(), calls=%async_computation.21 | async-start | bytes 17301504 | tf_op jit(solution)/shard_map/reduce_scatter | solution.py:381
  1319.8 2112.3 %reduce-scatter.33.cloned.1.call-start = ((), (), s32[]{:S(2)}) async-start(), calls=%async_computation.20 | async-start | bytes 17301504 | tf_op jit(solution)/shard_map/reduce_scatter | solution.py:381
  (34 other events, 48.5 us)
Sparse Core Ops, SparseCore 0:
  11.5 72.3 all-gather.34
  88.8 47.7 all-gather.28
  139.3 47.7 all-gather.26
  190.0 55.0 all-gather.36
  248.5 76.1 all-gather.38
  328.0 75.9 all-gather.40
  407.0 68.0 all-gather.42
  480.0 47.7 all-gather.32
  530.5 47.9 all-gather.30
  581.3 55.0 all-gather.44
  639.9 76.1 all-gather.46
  719.5 75.9 all-gather.48
  884.2 66.3 reduce-scatter.36
  954.0 66.7 reduce-scatter.38
  1116.3 66.6 reduce-scatter.40
  1186.4 66.6 reduce-scatter.42
  1259.9 122.2 all-reduce.15
  1384.3 144.6 reduce-scatter.26
  1531.3 141.8 reduce-scatter.24
  1679.0 153.0 reduce-scatter.46
  1839.2 154.4 reduce-scatter.44
  1996.0 357.1 reduce-scatter.30
  2355.5 357.3 reduce-scatter.28
  2715.0 357.3 reduce-scatter.34
  3074.7 357.3 reduce-scatter.32
where the time goes:
time: 3450 us; the launch traced here: 3440 us
  waiting for transfers between devices  2930 us (85%)
  matrix products  185 us (5%)
  local copies, waits for them, and re-layouts  163 us (5%)
  other arithmetic  80.6 us (2%)
  blocking collectives  62.1 us (2%)
    reduce_scatter x2, waiting for transfers between devices, body(): lax.psum_scatter(grad_second, ('dp', 'ctx'), scatter_dimension=0, tiled=T...  717 us
    reduce_scatter x2, waiting for transfers between devices, body(): lax.psum_scatter(grad_first, ('dp', 'ctx'), scatter_dimension=0, tiled=True)  716 us
    unnamed x32, waiting for transfers between devices  619 us
    reduce_scatter x2, waiting for transfers between devices, body(): lax.psum_scatter(grad_out_proj, ('dp', 'ctx'), scatter_dimension=0, tiled...  286 us
    all_gather x2, waiting for transfers between devices, body(): lax.all_gather(ffn_in_weight[layer], ('dp', 'ctx'), axis=0, tiled=True)  155 us
    all_gather x2, waiting for transfers between devices, body(): lax.all_gather(ffn_out_weight[layer], ('dp', 'ctx'), axis=0, tiled=True)  141 us
    all_gather x2, waiting for transfers between devices, body(): lax.all_gather(qkv_weight[layer], ('dp', 'ctx'), axis=0, tiled=True)  94.1 us
    all_gather x2, waiting for transfers between devices, body(): lax.all_gather(key_low, 'ctx', axis=0, tiled=True)  69.3 us
  transfers between devices with their start and end apart: 25, of which 25 were waited for; matrix products, arithmetic and copies ran while one was open for 6% of the time, Pallas kernels for 0%

commit v1 on v0

--- a/solution.py
+++ b/solution.py
@@ -1,11 +1,20 @@
+import math
+import types
+
 import jax
 import jax.numpy as jnp
 from jax import lax
+from jax.experimental import pallas as pl
+from jax.experimental.pallas import tpu as pltpu
 from jax.sharding import PartitionSpec as P
 
 ATTENTION_HEADS = 16
 
 
+DP, CTX = "dp", "ctx"
+BOTH = (DP, CTX)
+
+QUERY_KEY, TO_QUERY, TO_KEY = "qhd,khd->hqk", "hqk,khd->qhd", "hqk,qhd->khd"
 EPS = 1e-12
 NEGATIVE = -1e30
 
@@ -79,7 +88,7 @@
     seg_keys = lax.dynamic_slice_in_dim(segment_row, start, count, 0)
     mask = (seg_own[:, None] == seg_keys[None, :])[None]
     raw = (
-        jnp.einsum("qhd,khd->hqk", query_heads, split_key_heads, preferred_element_type=jnp.float32)
+        jnp.einsum(QUERY_KEY, query_heads, split_key_heads, preferred_element_type=jnp.float32)
         * scale
     )
     return (jnp.where(mask, raw, NEGATIVE), mask, split_key_heads)
@@ -105,19 +114,19 @@
     scale = head_width ** (-0.5)
     rows = hidden_in.shape[0]
     seg_own = document_index[0]
-    segment_row = lax.all_gather(document_index, "ctx", axis=1, tiled=True)[0]
+    segment_row = lax.all_gather(document_index, CTX, axis=1, tiled=True)[0]
     row_len = segment_row.shape[0]
     state = hidden_in.astype(jnp.float32)
     saved = []
     for layer in range(layers):
         fetched = (
-            lax.all_gather(qkv_weight[layer], ("dp", "ctx"), axis=0, tiled=True),
-            lax.all_gather(attention_output_weight[layer], ("dp", "ctx"), axis=0, tiled=True),
-            lax.all_gather(ffn_in_weight[layer], ("dp", "ctx"), axis=0, tiled=True),
-            lax.all_gather(ffn_out_weight[layer], ("dp", "ctx"), axis=0, tiled=True),
-            lax.all_gather(value_bias[layer], ("dp", "ctx"), axis=0, tiled=True),
-            lax.all_gather(biases[layer], ("dp", "ctx"), axis=0, tiled=True),
-            lax.all_gather(norm_gains[layer], ("dp", "ctx"), axis=0, tiled=True),
+            lax.all_gather(qkv_weight[layer], BOTH, axis=0, tiled=True),
+            lax.all_gather(attention_output_weight[layer], BOTH, axis=0, tiled=True),
+            lax.all_gather(ffn_in_weight[layer], BOTH, axis=0, tiled=True),
+            lax.all_gather(ffn_out_weight[layer], BOTH, axis=0, tiled=True),
+            lax.all_gather(value_bias[layer], BOTH, axis=0, tiled=True),
+            lax.all_gather(biases[layer], BOTH, axis=0, tiled=True),
+            lax.all_gather(norm_gains[layer], BOTH, axis=0, tiled=True),
         )
         (
             w_qkv,
@@ -158,7 +167,7 @@
         )
         held_pair = None
         top, total = by_blocks(
-            stats_step, stats_init, (lax.all_gather(key_low, "ctx", axis=0, tiled=True),), rows
+            stats_step, stats_init, (lax.all_gather(key_low, CTX, axis=0, tiled=True),), rows
         )
         log_total = top + jnp.log(total)
 
@@ -172,10 +181,10 @@
             probs_low = probs.astype(jnp.bfloat16)
             residue_low = (probs - probs_low.astype(jnp.float32)).astype(jnp.bfloat16)
             part_low = jnp.einsum(
-                "hqk,khd->qhd", probs_low, split_value_heads, preferred_element_type=jnp.float32
+                TO_QUERY, probs_low, split_value_heads, preferred_element_type=jnp.float32
             )
             part_fix = jnp.einsum(
-                "hqk,khd->qhd", residue_low, split_value_heads, preferred_element_type=jnp.float32
+                TO_QUERY, residue_low, split_value_heads, preferred_element_type=jnp.float32
             )
             return (context_acc + part_low, exact_acc + part_fix)
 
@@ -187,8 +196,8 @@
             value_step,
             value_init,
             (
-                lax.all_gather(key_low, "ctx", axis=0, tiled=True),
-                lax.all_gather(value_low, "ctx", axis=0, tiled=True),
+                lax.all_gather(key_low, CTX, axis=0, tiled=True),
+                lax.all_gather(value_low, CTX, axis=0, tiled=True),
             ),
             rows,
         )
@@ -240,13 +249,13 @@
             held_pair,
         ) = saved[layer]
         weights_now = (
-            lax.all_gather(qkv_weight[layer], ("dp", "ctx"), axis=0, tiled=True),
-            lax.all_gather(attention_output_weight[layer], ("dp", "ctx"), axis=0, tiled=True),
-            lax.all_gather(ffn_in_weight[layer], ("dp", "ctx"), axis=0, tiled=True),
-            lax.all_gather(ffn_out_weight[layer], ("dp", "ctx"), axis=0, tiled=True),
-            lax.all_gather(value_bias[layer], ("dp", "ctx"), axis=0, tiled=True),
-            lax.all_gather(biases[layer], ("dp", "ctx"), axis=0, tiled=True),
-            lax.all_gather(norm_gains[layer], ("dp", "ctx"), axis=0, tiled=True),
+            lax.all_gather(qkv_weight[layer], BOTH, axis=0, tiled=True),
+            lax.all_gather(attention_output_weight[layer], BOTH, axis=0, tiled=True),
+            lax.all_gather(ffn_in_weight[layer], BOTH, axis=0, tiled=True),
+            lax.all_gather(ffn_out_weight[layer], BOTH, axis=0, tiled=True),
+            lax.all_gather(value_bias[layer], BOTH, axis=0, tiled=True),
+            lax.all_gather(biases[layer], BOTH, axis=0, tiled=True),
+            lax.all_gather(norm_gains[layer], BOTH, axis=0, tiled=True),
         )
         (
             w_qkv,
@@ -296,7 +305,7 @@
             split_value_heads = parts[1].reshape(count, heads, head_width)
             probs = jnp.where(mask, jnp.exp(raw - log_total[:, :, None]), 0.0)
             back_probs = jnp.einsum(
-                "qhd,khd->hqk",
+                QUERY_KEY,
                 context_heads_back,
                 split_value_heads,
                 preferred_element_type=jnp.float32,
@@ -304,18 +313,18 @@
             back_scores = (probs * (back_probs - delta[:, :, None])).astype(jnp.bfloat16)
             query_part = (
                 jnp.einsum(
-                    "hqk,khd->qhd", back_scores, split_key_heads, preferred_element_type=jnp.float32
+                    TO_QUERY, back_scores, split_key_heads, preferred_element_type=jnp.float32
                 )
                 * scale
             )
             key_part = (
                 jnp.einsum(
-                    "hqk,qhd->khd", back_scores, query_heads, preferred_element_type=jnp.float32
+                    TO_KEY, back_scores, query_heads, preferred_element_type=jnp.float32
                 ).reshape(count, width)
                 * scale
             )
             value_part = jnp.einsum(
-                "hqk,qhd->khd",
+                TO_KEY,
                 probs.astype(jnp.bfloat16),
                 context_heads_back,
                 preferred_element_type=jnp.float32,
@@ -341,18 +350,18 @@
             grad_step,
             grad_init,
             (
-                lax.all_gather(key_low, "ctx", axis=0, tiled=True),
-                lax.all_gather(value_low, "ctx", axis=0, tiled=True),
+                lax.all_gather(key_low, CTX, axis=0, tiled=True),
+                lax.all_gather(value_low, CTX, axis=0, tiled=True),
             ),
             rows,
         )
         query_sum, key_sums, value_sums = folded
         key_own, value_own = (
             lax.psum_scatter(
-                key_sums.astype(jnp.bfloat16), "ctx", scatter_dimension=0, tiled=True
+                key_sums.astype(jnp.bfloat16), CTX, scatter_dimension=0, tiled=True
             ).astype(jnp.float32),
             lax.psum_scatter(
-                value_sums.astype(jnp.bfloat16), "ctx", scatter_dimension=0, tiled=True
+                value_sums.astype(jnp.bfloat16), CTX, scatter_dimension=0, tiled=True
             ).astype(jnp.float32),
         )
         back_qkv = jnp.concatenate(
@@ -374,13 +383,13 @@
         grad_gain = jnp.concatenate([back_gain_one, back_gain_two])
         upstream = back_one + back_product(back_qkv, w_qkv)
         shards = (
-            lax.psum_scatter(grad_qkv, ("dp", "ctx"), scatter_dimension=0, tiled=True),
-            lax.psum_scatter(grad_value_bias, ("dp", "ctx"), scatter_dimension=0, tiled=True),
-            lax.psum_scatter(grad_out_proj, ("dp", "ctx"), scatter_dimension=0, tiled=True),
-            lax.psum_scatter(grad_first, ("dp", "ctx"), scatter_dimension=0, tiled=True),
-            lax.psum_scatter(grad_second, ("dp", "ctx"), scatter_dimension=0, tiled=True),
-            lax.psum_scatter(grad_bias, ("dp", "ctx"), scatter_dimension=0, tiled=True),
-            lax.psum_scatter(grad_gain, ("dp", "ctx"), scatter_dimension=0, tiled=True),
+            lax.psum_scatter(grad_qkv, BOTH, scatter_dimension=0, tiled=True),
+            lax.psum_scatter(grad_value_bias, BOTH, scatter_dimension=0, tiled=True),
+            lax.psum_scatter(grad_out_proj, BOTH, scatter_dimension=0, tiled=True),
+            lax.psum_scatter(grad_first, BOTH, scatter_dimension=0, tiled=True),
+            lax.psum_scatter(grad_second, BOTH, scatter_dimension=0, tiled=True),
+            lax.psum_scatter(grad_bias, BOTH, scatter_dimension=0, tiled=True),
+            lax.psum_scatter(grad_gain, BOTH, scatter_dimension=0, tiled=True),
         )
         per_layer.append(shards)
     ordered = per_layer[::-1]
@@ -398,32 +407,1122 @@
     )
 
 
+MESH = pl.DeviceIdType.MESH
+F32 = jnp.float32
+BF16 = jnp.bfloat16
+VMEM = pltpu.VMEM
+ANY = pl.ANY
+VMEM_LIMIT = 56 * 2**20
+OWN, XN, YN, DIAG = range(4)
+
+
+def dot_nn(a, b):
+    return lax.dot_general(a, b, (((1,), (0,)), ((), ())), preferred_element_type=F32)
+
+
+def dot_nt(a, b):
+    return lax.dot_general(a, b, (((1,), (1,)), ((), ())), preferred_element_type=F32)
+
+
+def dot_tn(a, b):
+    return lax.dot_general(a, b, (((0,), (0,)), ((), ())), preferred_element_type=F32)
+
+
+def place():
+    d, t = lax.axis_index(DP), lax.axis_index(CTX)
+    x, c = lax.div(d, 2), lax.rem(d, 2)
+    z, y = lax.div(t, 2), lax.rem(t, 2)
+    w = types.SimpleNamespace(d=d, x=x, c=c, z=z, y=y)
+    w.part = d * 2 + y
+    w.group = (x * 2 + y, (1 - x) * 2 + y, x * 2 + 1 - y, (1 - x) * 2 + 1 - y)
+    w.xn, w.yn, w.sib = ((1 - x) * 2 + c, t), (d, z * 2 + 1 - y), (x * 2 + 1 - c, t)
+    w.zs = [(d, lax.rem(z + k, 4) * 2 + y) for k in (1, 2, 3)]
+    w.plane = []
+    for bits in range(1, 8):
+        xx = 1 - x if bits & 4 else x
+        cc = 1 - c if bits & 2 else c
+        yy = 1 - y if bits & 1 else y
+        w.plane.append(((xx * 2 + cc, z * 2 + yy), (xx * 2 + cc) * 2 + yy))
+    w.swap = (z, d * 2 + y)
+    return w
+
+
+class Net:
+    def __init__(self, ssem, rsem, lsem):
+        self.ssem, self.rsem, self.lsem = ssem, rsem, lsem
+        self.sent, self.kept, self.swaps = [], [], []
+        self.at = 0
+
+    def greet(self, devices, w, swap=False):
+        barrier = pltpu.get_barrier_semaphore()
+        for device in devices:
+            pl.semaphore_signal(barrier, inc=1, device_id=device, device_id_type=MESH)
+        more = 0
+        if swap:
+            more = jnp.where(w.d != w.z, 1, 0)
+
+            @pl.when(w.d != w.z)
+            def _():
+                pl.semaphore_signal(barrier, inc=1, device_id=w.swap, device_id_type=MESH)
+
+        pl.semaphore_wait(barrier, len(devices) + more)
+
+    def make(self, src, dst, device):
+        copy = pltpu.make_async_remote_copy(
+            src_ref=src,
+            dst_ref=dst,
+            send_sem=self.ssem.at[self.at],
+            recv_sem=self.rsem.at[self.at],
+            device_id=device,
+            device_id_type=MESH,
+        )
+        self.at += 1
+        return copy
+
+    def send(self, src, dst, device):
+        copy = self.make(src, dst, device)
+        copy.start()
+        self.sent.append(copy)
+        return copy
+
+    def local(self, src, dst):
+        copy = pltpu.make_async_copy(src, dst, self.lsem.at[len(self.kept)])
+        copy.start()
+        self.kept.append(copy)
+        return copy
+
+    def swap(self, w, src, dst):
+        far = self.make(src, dst, w.swap)
+        near = pltpu.make_async_copy(src, dst, self.lsem.at[len(self.kept)])
+        self.kept.append(None)
+
+        @pl.when(w.d != w.z)
+        def _():
+            far.start()
+
+        @pl.when(w.d == w.z)
+        def _():
+            near.start()
+
+        def wait():
+            @pl.when(w.d != w.z)
+            def _():
+                far.wait()
+
+            @pl.when(w.d == w.z)
+            def _():
+                near.wait()
+
+        return wait
+
+    def z_gather(self, w, src, at):
+        copies = [self.send(src, at(w.z), device) for device in w.zs]
+        own = self.local(src, at(w.z))
+
+        def wait():
+            own.wait()
+            for copy in copies:
+                copy.wait_recv()
+
+        return wait
+
+    def z_scatter(self, w, at, land):
+        copies = [
+            self.send(at(lax.rem(w.z + k + 1, 4)), land.at[k], device)
+            for k, device in enumerate(w.zs)
+        ]
+        own = self.local(at(w.z), land.at[3])
+
+        def wait():
+            own.wait()
+            for copy in copies:
+                copy.wait_recv()
+
+        return wait
+
+    def plane_swap(self, w, at, to):
+        copies = [self.send(at(part), to(w.part), device) for device, part in w.plane]
+        own = self.local(at(w.part), to(w.part))
+
+        def wait():
+            own.wait()
+            for copy in copies:
+                copy.wait_recv()
+
+        return wait
+
+    def finish(self):
+        for copy in self.sent:
+            copy.wait_send()
+
+
+def gather(net, w, buf, on_group, after_start):
+    def half(group, h):
+        return buf.at[pl.ds(pl.multiple_of((group * 2 + w.c) * 128 + h * 64, 64), 64)]
+
+    def put(group, h, device):
+        ref = half(group, h)
+        return net.send(ref, ref, device)
+
+    own, xn, yn, diag = w.group
+    x0 = put(own, 0, w.xn)
+    y1 = put(own, 1, w.yn)
+    whole = buf.at[pl.ds(pl.multiple_of((own * 2 + w.c) * 128, 128), 128)]
+    c0 = net.send(whole, whole, w.sib)
+    x1 = put(own, 1, w.xn)
+    y0 = put(own, 0, w.yn)
+    after_start()
+    c0.wait_recv()
+    on_group(OWN)
+    x0.wait_recv()
+    d0 = put(xn, 0, w.yn)
+    cx0 = put(xn, 0, w.sib)
+    y1.wait_recv()
+    d1 = put(yn, 1, w.xn)
+    cy1 = put(yn, 1, w.sib)
+    x1.wait_recv()
+    cx1 = put(xn, 1, w.sib)
+    y0.wait_recv()
+    cy0 = put(yn, 0, w.sib)
+    cx0.wait_recv()
+    cx1.wait_recv()
+    on_group(XN)
+    cy0.wait_recv()
+    cy1.wait_recv()
+    on_group(YN)
+    d0.wait_recv()
+    cd0 = put(diag, 0, w.sib)
+    d1.wait_recv()
+    cd1 = put(diag, 1, w.sib)
+    cd0.wait_recv()
+    cd1.wait_recv()
+    on_group(DIAG)
+
+
+class Reduce:
+    def __init__(self, net, w, r, part):
+        self.net, self.w, self.r, self.part = net, w, r, part
+        self.cores = dict()
+
+    def produce(self, kind):
+        w, r, k = self.w, self.r, kind
+        group = w.group[kind]
+        r.core_out[k] = self.part(group * 2 + 1 - w.c).astype(BF16)
+        self.cores[kind] = self.net.send(r.core_out.at[k], r.core_in.at[k], w.sib)
+        r.keep[k] = self.part(group * 2 + w.c)
+
+    def diag(self):
+        w, r = self.w, self.r
+        self.cores[DIAG].wait_recv()
+        r.far[...] = (r.keep[3] + r.core_in[3].astype(F32)).astype(BF16)
+        self.fy = self.net.send(r.far.at[pl.ds(0, 64)], r.via_y, w.yn)
+        self.fx = self.net.send(r.far.at[pl.ds(64, 64)], r.via_x, w.xn)
+
+    def first(self):
+        w, r = self.w, self.r
+        self.cores[XN].wait_recv()
+        r.out_x[64:128] = (r.keep[1, 64:128] + r.core_in[1, 64:128].astype(F32)).astype(BF16)
+        self.x1 = self.net.send(r.out_x.at[pl.ds(64, 64)], r.in_x.at[pl.ds(64, 64)], w.xn)
+        self.cores[YN].wait_recv()
+        r.out_y[0:64] = (r.keep[2, 0:64] + r.core_in[2, 0:64].astype(F32)).astype(BF16)
+        self.y0 = self.net.send(r.out_y.at[pl.ds(0, 64)], r.in_y.at[pl.ds(0, 64)], w.yn)
+
+    def second(self):
+        w, r = self.w, self.r
+        self.fy.wait_recv()
+        r.out_x[0:64] = (
+            r.keep[1, 0:64] + r.core_in[1, 0:64].astype(F32) + r.via_y[...].astype(F32)
+        ).astype(BF16)
+        self.x0 = self.net.send(r.out_x.at[pl.ds(0, 64)], r.in_x.at[pl.ds(0, 64)], w.xn)
+        self.fx.wait_recv()
+        r.out_y[64:128] = (
+            r.keep[2, 64:128] + r.core_in[2, 64:128].astype(F32) + r.via_x[...].astype(F32)
+        ).astype(BF16)
+        self.y1 = self.net.send(r.out_y.at[pl.ds(64, 64)], r.in_y.at[pl.ds(64, 64)], w.yn)
+
+    def total(self):
+        r = self.r
+        self.cores[OWN].wait_recv()
+        for copy in (self.x1, self.y0, self.x0, self.y1):
+            copy.wait_recv()
+        return (
+            r.keep[0] + r.core_in[0].astype(F32) + r.in_x[...].astype(F32) + r.in_y[...].astype(F32)
+        )
+
+
+def reduce_scratch(width):
+    return dict(
+        core_out=VMEM((4, 128, width), BF16),
+        core_in=VMEM((4, 128, width), BF16),
+        keep=VMEM((4, 128, width), F32),
+        far=VMEM((128, width), BF16),
+        via_x=VMEM((64, width), BF16),
+        via_y=VMEM((64, width), BF16),
+        out_x=VMEM((128, width), BF16),
+        out_y=VMEM((128, width), BF16),
+        in_x=VMEM((128, width), BF16),
+        in_y=VMEM((128, width), BF16),
+    )
+
+
+def run(body, ins, outs, scratch, number, flops=0):
+    names = [*ins, *outs, *scratch]
+
+    def kernel(*refs):
+        r = types.SimpleNamespace(**dict(zip(names, refs)))
+        net = Net(*refs[len(names) :])
+        body(net, place(), r)
+        net.finish()
+
+    results = pl.pallas_call(
+        kernel,
+        out_shape=[jax.ShapeDtypeStruct(shape, dtype) for shape, dtype, _ in outs.values()],
+        in_specs=[pl.BlockSpec(memory_space=memory) for _, memory in ins.values()],
+        out_specs=[pl.BlockSpec(memory_space=memory) for _, _, memory in outs.values()],
+        scratch_shapes=[
+            *scratch.values(),
+            pltpu.SemaphoreType.DMA((80,)),
+            pltpu.SemaphoreType.DMA((80,)),
+            pltpu.SemaphoreType.DMA((16,)),
+        ],
+        compiler_params=pltpu.CompilerParams(
+            collective_id=number, has_side_effects=True, vmem_limit_bytes=VMEM_LIMIT
+        ),
+        cost_estimate=pl.CostEstimate(flops=flops, bytes_accessed=8 * 2**20, transcendentals=0),
+    )(*[array for array, _ in ins.values()])
+    return types.SimpleNamespace(**dict(zip(outs, results)))
+
+
+def neighbours(w):
+    return [w.xn, w.yn, w.sib, *w.zs]
+
+
+def bringing(**items):
+    every = dict(swap=None, qkv=None, out=None, plane=None, inner=None, ffo=None)
+    return types.SimpleNamespace(**dict(every, **items))
+
+
+def rows_of(group, n=256):
+    return pl.ds(pl.multiple_of(group * n, n), n)
+
+
+def norm_parts(resid):
+    mean = jnp.mean(resid, axis=-1, keepdims=True)
+    centered = resid - mean
+    variance = jnp.mean(centered * centered, axis=-1, keepdims=True)
+    root = lax.rsqrt(variance + EPS)
+    return centered * root, root
+
+
+def norm_back(grad, hat, root, gain):
+    scaled = grad * gain
+    return root * (
+        scaled
+        - jnp.mean(scaled, axis=-1, keepdims=True)
+        - hat * jnp.mean(scaled * hat, axis=-1, keepdims=True)
+    )
+
+
+def column_sum(value):
+    return jnp.sum(value, axis=0, keepdims=True)
+
+
+def of_head(value, h):
+    lanes = lax.broadcasted_iota(jnp.int32, value.shape, 1)
+    keep = lanes < 64 if h == 0 else lanes >= 64
+    return jnp.where(keep, value, jnp.zeros_like(value))
+
+
+G1, S1, BO, G2, S2, B2 = range(6)
+
+
+def start_kernel(sent, number):
+    layers = 2
+    three, ff = sent.qkv.shape[-1], sent.inner.shape[-1]
+    width = sent.hidden.shape[1]
+
+    def body(net, w, r):
+        net.greet([dev for dev, _ in w.plane] + w.zs, w, swap=True)
+        hidden = net.swap(w, r.hidden, r.hidden_row)
+        docs = net.swap(w, r.docs, r.docs_own)
+        first = net.plane_swap(w, lambda p: r.qkv.at[0, p], lambda p: r.qkv_zero.at[p])
+        vec = net.z_gather(w, r.vec, lambda z: r.vec_z.at[z])
+        out = net.z_gather(w, r.out, lambda z: r.out_all.at[z])
+        vec()
+        vec_all = net.plane_swap(w, lambda p: r.vec_z, lambda p: r.vec_all.at[p])
+        first()
+        copies = [
+            net.send(r.qkv_zero.at[pl.ds(2 * k, 2)], r.qkv_all.at[k, w.z], device)
+            for device in w.zs
+            for k in range(4)
+        ]
+        own = [net.local(r.qkv_zero.at[pl.ds(2 * k, 2)], r.qkv_all.at[k, w.z]) for k in range(4)]
+        later = [net.plane_swap(w, lambda p: r.qkv.at[1, p], lambda p: r.qkv_one.at[p])]
+        for layer in range(layers):
+            later.append(
+                net.plane_swap(
+                    w,
+                    lambda p, layer=layer: r.inner.at[layer, p],
+                    lambda p, layer=layer: r.inner_z.at[layer, p],
+                )
+            )
+        docs()
+        spread = net.plane_swap(w, lambda p: r.docs_own, lambda p: r.docs_all.at[p])
+        hidden()
+        for wait in later:
+            wait()
+        out()
+        vec_all()
+        spread()
+        for copy in own:
+            copy.wait()
+        for copy in copies:
+            copy.wait_recv()
+
+    return run(
+        body,
+        dict(
+            hidden=(sent.hidden, ANY),
+            docs=(sent.docs, VMEM),
+            vec=(sent.vec, VMEM),
+            qkv=(sent.qkv, ANY),
+            inner=(sent.inner, ANY),
+            out=(sent.out, ANY),
+        ),
+        dict(
+            hidden_row=((128, width), BF16, ANY),
+            docs_all=((8, 8, 128), jnp.int32, ANY),
+            vec_all=((8, 4, 16, 128), BF16, ANY),
+            qkv_one=((8, 32, three), BF16, ANY),
+            inner_z=((layers, 8, 32, ff), BF16, ANY),
+            qkv_all=((4, 4, 2, 32, three), BF16, ANY),
+            out_all=((4, 32, width), BF16, ANY),
+        ),
+        dict(
+            docs_own=VMEM((8, 128), jnp.int32),
+            vec_z=VMEM((4, 16, 128), BF16),
+            qkv_zero=VMEM((8, 32, three), BF16),
+        ),
+        number,
+    )
+
+
+def attend_kernel(state, low, weights, out_z, docs, vec, tpb, bring, number):
+    width = low.shape[1]
+    scale = (width // ATTENTION_HEADS) ** (-0.5)
+
+    def body(net, w, r):
+        net.greet(neighbours(w), w)
+        r.all_low[pl.ds(pl.multiple_of((w.group[OWN] * 2 + w.c) * 128, 128), 128)] = r.low[...]
+        waits = []
+        extra = types.SimpleNamespace()
+
+        def after_start():
+            extra.out = net.send(
+                r.out_z.at[pl.ds(2 * (1 - w.y), 2)], r.out_w.at[:, w.y], w.yn
+            )
+            extra.own = net.local(r.out_z.at[pl.ds(2 * w.y, 2)], r.out_w.at[:, w.y])
+            waits.append(
+                net.z_gather(w, r.b_inner, lambda z: r.inner_all.at[:, z])
+            )
+            waits.append(net.z_gather(w, r.b_ffo, lambda z: r.ffo_all.at[z]))
+
+        bias = r.tpb[0:1, 0 : r.weights.shape[1]]
+
+        def on_group(kind):
+            rows = rows_of(w.group[kind])
+            r.qkv[rows] = (dot_nn(r.all_low[rows], r.weights[...]) + bias).astype(BF16)
+
+        gather(net, w, r.all_low, on_group, after_start)
+        value = r.qkv[:, 256:384]
+        for h in range(2):
+            r.split_v[h] = of_head(value, h)
+        extra.out.wait_recv()
+        extra.own.wait()
+
+        def attend(kind):
+            def block(i, carry):
+                rows = pl.ds(pl.multiple_of(w.group[kind] * 256 + i * 128, 128), 128)
+                query = r.qkv[rows, 0:128]
+                mask = r.docs_col[rows, 0:1] == r.docs_row[0:1, :]
+                total, logs = None, []
+                for h in range(2):
+                    raw = dot_nt(of_head(query, h), r.qkv[:, 128:256]) * scale
+                    raw = jnp.where(mask, raw, NEGATIVE)
+                    top = jnp.max(raw, axis=-1, keepdims=True)
+                    weight = jnp.exp(raw - top)
+                    mass = jnp.sum(weight, axis=-1, keepdims=True)
+                    probs = (weight * (1.0 / mass)).astype(BF16)
+                    piece = dot_nn(probs, r.split_v[h])
+                    total = piece if total is None else total + piece
+                    logs.append(top + jnp.log(mass))
+                r.context[rows] = total.astype(BF16)
+                lanes = lax.broadcasted_iota(jnp.int32, (128, 128), 1)
+                r.logs[rows] = jnp.where(lanes < 64, logs[0], logs[1])
+                return carry
+
+            lax.fori_loop(0, 2, block, 0)
+
+        out_w = r.out_w
+
+        def part(slot):
+            return dot_nn(r.context[rows_of(slot, 128)], out_w[...].reshape(128, width))
+
+        reduce = Reduce(net, w, r, part)
+        for kind in (DIAG, XN):
+            attend(kind)
+            reduce.produce(kind)
+        reduce.diag()
+        attend(YN)
+        reduce.produce(YN)
+        reduce.first()
+        attend(OWN)
+        reduce.produce(OWN)
+        reduce.second()
+        before = r.low[...].astype(F32) if state is None else r.state[...]
+        hat, root = norm_parts(before + reduce.total() + r.vec[BO : BO + 1])
+        normed = hat * r.vec[G1 : G1 + 1] + r.vec[S1 : S1 + 1]
+        r.normed[...] = normed
+        r.normed_low[...] = normed.astype(BF16)
+        r.hat[...] = hat
+        r.root[...] = jnp.broadcast_to(root, (128, 128))
+        for wait in waits:
+            wait()
+
+    ff = bring.inner.shape[-1]
+    ins = dict(
+        low=(low, VMEM),
+        weights=(weights, VMEM),
+        out_z=(out_z, VMEM),
+        docs_row=(docs[0], VMEM),
+        docs_col=(docs[1], VMEM),
+        vec=(vec, VMEM),
+        tpb=(tpb, VMEM),
+        b_inner=(bring.inner, ANY),
+        b_ffo=(bring.ffo, ANY),
+    )
+    if state is not None:
+        ins.update(state=(state, VMEM))
+    return run(
+        body,
+        ins,
+        dict(
+            all_low=((1024, width), BF16, VMEM),
+            qkv=((1024, 384), BF16, VMEM),
+            context=((1024, 128), BF16, VMEM),
+            logs=((1024, 128), F32, VMEM),
+            out_w=((2, 2, 32, width), BF16, VMEM),
+            normed=((128, width), F32, VMEM),
+            normed_low=((128, width), BF16, VMEM),
+            hat=((128, width), F32, VMEM),
+            root=((128, 128), F32, VMEM),
+            inner_all=((4, 4, 64, ff), BF16, ANY),
+            ffo_all=((4, 128, width), BF16, ANY),
+        ),
+        dict(split_v=VMEM((2, 1024, 128), BF16), **reduce_scratch(width)),
+        number,
+    )
+
+
+def feed_kernel(normed, low, w_in, w_ffo, vec, tpb, bring, number):
+    width, ff = low.shape[1], w_in.shape[1]
+
+    def body(net, w, r):
+        net.greet(neighbours(w), w, swap=bring.swap is not None)
+        r.all_low[pl.ds(pl.multiple_of((w.group[OWN] * 2 + w.c) * 128, 128), 128)] = r.low[...]
+        waits = []
+
+        def after_start():
+            if bring.swap is not None:
+                waits.append(net.swap(w, r.b_swap, r.swapped))
+            if bring.qkv is not None:
+                waits.append(net.z_gather(w, r.b_out, lambda z: r.out_all.at[z]))
+                waits.append(net.z_gather(w, r.b_qkv, lambda z: r.qkv_all.at[:, z]))
+
+        bias = r.tpb[1:2, 0:ff]
+
+        def part(slot):
+            return dot_nn(r.inner[rows_of(slot, 128)], r.w_ffo[...])
+
+        reduce = Reduce(net, w, r, part)
+
+        def on_group(kind):
+            r.pre[...] = dot_nn(r.all_low[rows_of(w.group[kind])], r.w_in[...]) + bias
+
+            def block(i, carry):
+                here = pl.ds(pl.multiple_of(i * 32, 32), 32)
+                there = pl.ds(pl.multiple_of(w.group[kind] * 256 + i * 32, 32), 32)
+                pre = r.pre[here]
+                cdf = 0.5 * (1.0 + lax.erf(pre * (0.5**0.5)))
+                r.inner[there] = (pre * cdf).astype(BF16)
+                bell = jnp.exp(pre * pre * (-0.5)) * ((2.0 * math.pi) ** (-0.5))
+                r.slope[there] = cdf + pre * bell
+                return carry
+
+            lax.fori_loop(0, 8, block, 0)
+            reduce.produce(kind)
+            if kind == YN:
+                reduce.first()
+
+        gather(net, w, r.all_low, on_group, after_start)
+        reduce.diag()
+        reduce.second()
+        hat, root = norm_parts(r.normed[...] + reduce.total() + r.vec[B2 : B2 + 1])
+        state = hat * r.vec[G2 : G2 + 1] + r.vec[S2 : S2 + 1]
+        r.state[...] = state
+        r.state_low[...] = state.astype(BF16)
+        r.hat[...] = hat
+        r.root[...] = jnp.broadcast_to(root, (128, 128))
+        for wait in waits:
+            wait()
+
+    ins = dict(
+        normed=(normed, VMEM),
+        low=(low, VMEM),
+        w_in=(w_in, VMEM),
+        w_ffo=(w_ffo, VMEM),
+        vec=(vec, VMEM),
+        tpb=(tpb, VMEM),
+    )
+    outs = dict(
+        all_low=((1024, width), BF16, VMEM),
+        inner=((1024, ff), BF16, VMEM),
+        slope=((1024, ff), F32, VMEM),
+        state=((128, width), F32, VMEM),
+        state_low=((128, width), BF16, VMEM),
+        hat=((128, width), F32, VMEM),
+        root=((128, 128), F32, VMEM),
+    )
+    if bring.swap is not None:
+        ins.update(b_swap=(bring.swap, ANY))
+        outs.update(swapped=((128, width), BF16, ANY))
+    if bring.qkv is not None:
+        ins.update(b_out=(bring.out, ANY))
+        ins.update(b_qkv=(bring.qkv, ANY))
+        outs.update(out_all=((4, 32, width), BF16, ANY))
+        outs.update(qkv_all=((4, 4, 64, bring.qkv.shape[-1]), BF16, ANY))
+    return run(body, ins, outs, dict(pre=VMEM((256, ff), F32), **reduce_scratch(width)), number)
+
+
+def feed_back_kernel(grad, saved, hat_one, root_one, w_in, w_ffo, vec, bring, number):
+    width, ff = hat_one.shape[1], w_in.shape[1]
+
+    def body(net, w, r):
+        plane = bring.plane is not None
+        net.greet(
+            [dev for dev, _ in w.plane] + w.zs if plane else neighbours(w), w, swap=bring.swap is not None
+        )
+        grad = r.grad[...].astype(F32)
+        hat = r.hat_two[...]
+        back_two = norm_back(grad, hat, r.root_two[:, 0:1], r.vec[G2 : G2 + 1])
+        second = back_two.astype(BF16)
+        r.back_two[...] = back_two
+        r.all_back[pl.ds(pl.multiple_of((w.group[OWN] * 2 + w.c) * 128, 128), 128)] = second
+        r.sums[...] = jnp.zeros_like(r.sums)
+        r.sums[G2 : G2 + 1, :] = column_sum(grad * hat)
+        r.sums[S2 : S2 + 1, :] = column_sum(grad)
+        r.sums[B2 : B2 + 1, :] = column_sum(second.astype(F32))
+        waits = []
+
+        def after_start():
+            if bring.swap is not None:
+                waits.append(net.swap(w, r.b_swap, r.swapped))
+            if bring.qkv is not None:
+                waits.append(net.z_scatter(w, lambda z: r.b_out.at[z], r.land_out))
+                waits.append(net.z_scatter(w, lambda z: r.b_qkv.at[:, z], r.land_qkv))
+            if plane:
+                waits.append(
+                    net.plane_swap(w, lambda p: r.b_plane.at[p], lambda p: r.plane_all.at[p])
+                )
+
+        def part(slot):
+            return dot_nt(r.back_pre[rows_of(slot, 128)], r.w_in[...])
+
+        reduce = Reduce(net, w, r, part)
+
+        def on_group(kind):
+            rows = rows_of(w.group[kind])
+            back_inner = dot_nt(r.all_back[rows], r.w_ffo[...])
+            r.back_pre[rows] = (back_inner * r.slope[rows]).astype(BF16)
+            reduce.produce(kind)
+            if kind == YN:
+                reduce.first()
+
+        gather(net, w, r.all_back, on_group, after_start)
+        reduce.diag()
+
+        def ffo_block(i, carry):
+            lanes = pl.ds(pl.multiple_of(i * 128, 128), 128)
+            r.g_ffo[lanes] = dot_tn(r.inner[:, lanes], r.all_back[...]).astype(BF16)
+            return carry
+
+        lax.fori_loop(0, ff // 128, ffo_block, 0)
+        reduce.second()
+
+        def in_block(i, carry):
+            lanes = pl.ds(pl.multiple_of(i * 128, 128), 128)
+            r.g_in[lanes] = dot_tn(r.all_low[:, lanes], r.back_pre[...]).astype(BF16)
+            return carry
+
+        lax.fori_loop(0, width // 128, in_block, 0)
+        r.sums[6:7, 256 : 256 + ff] = column_sum(r.back_pre[...].astype(F32))
+        grad_one = r.back_two[...] + reduce.total()
+        hat = r.hat_one[...]
+        back_one = norm_back(grad_one, hat, r.root_one[:, 0:1], r.vec[G1 : G1 + 1])
+        branch = back_one.astype(BF16)
+        r.back_one[...] = back_one
+        r.branch[...] = branch
+        r.sums[G1 : G1 + 1, :] = column_sum(grad_one * hat)
+        r.sums[S1 : S1 + 1, :] = column_sum(grad_one)
+        r.sums[BO : BO + 1, :] = column_sum(branch.astype(F32))
+        for wait in waits:
+            wait()
+        if bring.qkv is not None:
+            r.red_out[...] = sum(r.land_out[k].astype(F32) for k in range(4))
+            r.red_qkv[...] = sum(r.land_qkv[k].astype(F32) for k in range(4)).astype(BF16)
+
+    ins = dict(
+        grad=(grad, VMEM),
+        hat_two=(saved.hat, VMEM),
+        root_two=(saved.root, VMEM),
+        all_low=(saved.all_low, VMEM),
+        inner=(saved.inner, VMEM),
+        slope=(saved.slope, VMEM),
+        hat_one=(hat_one, VMEM),
+        root_one=(root_one, VMEM),
+        w_in=(w_in, VMEM),
+        w_ffo=(w_ffo, VMEM),
+        vec=(vec, VMEM),
+    )
+    outs = dict(
+        g_ffo=((ff, width), BF16, VMEM),
+        g_in=((width, ff), BF16, VMEM),
+        back_one=((128, width), F32, VMEM),
+        branch=((128, width), BF16, VMEM),
+        sums=((8, width), F32, VMEM),
+    )
+    scratch = dict(
+        all_back=VMEM((1024, width), BF16),
+        back_two=VMEM((128, width), F32),
+        back_pre=VMEM((1024, ff), BF16),
+        **reduce_scratch(width),
+    )
+    if bring.swap is not None:
+        ins.update(b_swap=(bring.swap, ANY))
+        outs.update(swapped=((128, width), BF16, ANY))
+    if bring.qkv is not None:
+        ins.update(b_out=(bring.out, ANY))
+        ins.update(b_qkv=(bring.qkv, ANY))
+        outs.update(red_out=((32, width), F32, VMEM))
+        outs.update(red_qkv=((4, 64, 384), BF16, VMEM))
+        scratch.update(land_out=VMEM((4, 32, width), BF16))
+        scratch.update(land_qkv=VMEM((4, 4, 64, 384), BF16))
+    if bring.plane is not None:
+        ins.update(b_plane=(bring.plane, ANY))
+        outs.update(plane_all=(bring.plane.shape, BF16, ANY))
+    return run(body, ins, outs, scratch, number)
+
+
+def attend_back_kernel(back_one, branch, saved, weights, docs, bring, number):
+    width = branch.shape[1]
+    ff = bring.inner.shape[-1]
+    scale = (width // ATTENTION_HEADS) ** (-0.5)
+
+    def body(net, w, r):
+        plane = bring.plane is not None
+        net.greet([dev for dev, _ in w.plane] + w.zs if plane else neighbours(w), w)
+        r.all_back[pl.ds(pl.multiple_of((w.group[OWN] * 2 + w.c) * 128, 128), 128)] = r.branch[...]
+        r.sum_k[...] = jnp.zeros_like(r.sum_k)
+        r.sum_v[...] = jnp.zeros_like(r.sum_v)
+        key = r.qkv[:, 128:256]
+        for h in range(2):
+            r.split_k[h] = of_head(key, h)
+        waits = []
+
+        def after_start():
+            waits.append(net.z_scatter(w, lambda z: r.b_ffo.at[z], r.land_ffo))
+            waits.append(net.z_scatter(w, lambda z: r.b_inner.at[:, z], r.land_in))
+            if plane:
+                waits.append(
+                    net.plane_swap(w, lambda p: r.b_plane.at[p], lambda p: r.plane_all.at[p])
+                )
+
+        def on_group(kind):
+            rows = rows_of(w.group[kind])
+            r.back_context[rows] = dot_nt(r.all_back[rows], r.out_w[...].reshape(128, width)).astype(BF16)
+
+            def block(i, carry):
+                here = pl.ds(pl.multiple_of(w.group[kind] * 256 + i * 128, 128), 128)
+                query = r.qkv[here, 0:128]
+                upstream = r.back_context[here]
+                mask = r.docs_col[here, 0:1] == r.docs_row[0:1, :]
+                total = None
+                for h in range(2):
+                    query_h, upstream_h = of_head(query, h), of_head(upstream, h)
+                    raw = dot_nt(query_h, r.qkv[:, 128:256]) * scale
+                    raw = jnp.where(mask, raw, NEGATIVE)
+                    probs = jnp.exp(raw - r.logs[here, h * 64 : h * 64 + 1])
+                    back = dot_nt(upstream_h, r.qkv[:, 256:384])
+                    delta = jnp.sum(probs * back, axis=-1, keepdims=True)
+                    scores = (probs * (back - delta)).astype(BF16)
+                    piece = dot_nn(scores, r.split_k[h])
+                    total = piece if total is None else total + piece
+                    r.sum_k[...] += dot_tn(scores, query_h)
+                    r.sum_v[...] += dot_tn(probs.astype(BF16), upstream_h)
+                r.back_qkv[here, 0:128] = (total * scale).astype(BF16)
+                return carry
+
+            lax.fori_loop(0, 2, block, 0)
+
+        gather(net, w, r.all_back, on_group, after_start)
+        r.back_qkv[:, 128:256] = (r.sum_k[...] * scale).astype(BF16)
+        r.back_qkv[:, 256:384] = r.sum_v[...].astype(BF16)
+
+        def part(slot):
+            return dot_nt(r.back_qkv[rows_of(slot, 128)], r.weights[...])
+
+        reduce = Reduce(net, w, r, part)
+        reduce.produce(DIAG)
+        reduce.produce(XN)
+        reduce.diag()
+        reduce.produce(YN)
+        reduce.first()
+        reduce.produce(OWN)
+        r.g_out[...] = dot_tn(r.context[...], r.all_back[...]).astype(BF16).reshape(2, 2, 32, width)
+        cross_y = net.send(r.g_out.at[:, 1 - w.y], r.g_out_z.at[pl.ds(2 * w.y, 2)], w.yn)
+        kept = net.local(r.g_out.at[:, w.y], r.g_out_z.at[pl.ds(2 * w.y, 2)])
+        reduce.second()
+
+        def qkv_block(i, carry):
+            lanes = pl.ds(pl.multiple_of(i * 128, 128), 128)
+            r.g_qkv[lanes] = dot_tn(r.all_low[:, lanes], r.back_qkv[...]).astype(BF16)
+            return carry
+
+        lax.fori_loop(0, width // 128, qkv_block, 0)
+        r.sums[...] = jnp.zeros_like(r.sums)
+        r.sums[0:1, 0:384] = column_sum(r.back_qkv[...].astype(F32))
+        r.grad[...] = r.back_one[...] + reduce.total()
+        for wait in waits:
+            wait()
+        kept.wait()
+        cross_y.wait_recv()
+        r.red_ffo[...] = sum(r.land_ffo[k].astype(F32) for k in range(4))
+        r.red_in[...] = sum(r.land_in[k].astype(F32) for k in range(4)).astype(BF16)
+
+    ins = dict(
+        back_one=(back_one, VMEM),
+        branch=(branch, VMEM),
+        qkv=(saved.qkv, VMEM),
+        context=(saved.context, VMEM),
+        logs=(saved.logs, VMEM),
+        all_low=(saved.all_low, VMEM),
+        out_w=(saved.out_w, VMEM),
+        weights=(weights, VMEM),
+        docs_row=(docs[0], VMEM),
+        docs_col=(docs[1], VMEM),
+        b_ffo=(bring.ffo, ANY),
+        b_inner=(bring.inner, ANY),
+    )
+    outs = dict(
+        grad=((128, width), F32, VMEM),
+        g_qkv=((width, 384), BF16, VMEM),
+        g_out_z=((4, 32, width), BF16, VMEM),
+        sums=((8, 384), F32, VMEM),
+        red_ffo=((128, width), F32, VMEM),
+        red_in=((4, 64, ff), BF16, VMEM),
+    )
+    scratch = dict(
+        all_back=VMEM((1024, width), BF16),
+        sum_k=VMEM((1024, 128), F32),
+        sum_v=VMEM((1024, 128), F32),
+        split_k=VMEM((2, 1024, 128), BF16),
+        back_context=VMEM((1024, 128), BF16),
+        back_qkv=VMEM((1024, 384), BF16),
+        g_out=VMEM((2, 2, 32, width), BF16),
+        land_ffo=VMEM((4, 128, width), BF16),
+        land_in=VMEM((4, 4, 64, ff), BF16),
+        **reduce_scratch(width),
+    )
+    if bring.plane is not None:
+        ins.update(b_plane=(bring.plane, ANY))
+        outs.update(plane_all=(bring.plane.shape, BF16, ANY))
+    return run(body, ins, outs, scratch, number)
+
+
+def end_kernel(grad_low, g_qkv, g_out, red_in, vecs, number):
+    width, ff = grad_low.shape[1], red_in.shape[-1]
+
+    def body(net, w, r):
+        net.greet([dev for dev, _ in w.plane] + w.zs, w, swap=True)
+        qkv = net.z_scatter(w, lambda z: r.qkv.at[:, z], r.land_qkv)
+        out = net.z_scatter(w, lambda z: r.out.at[z], r.land_out)
+        vec = net.z_scatter(w, lambda z: r.vecs, r.land_vec)
+        grad = net.swap(w, r.grad_low, r.grad)
+        inner = net.plane_swap(w, lambda p: r.inner.at[p], lambda p: r.g_in.at[p])
+        vec()
+        r.vec_z[...] = r.land_vec[0] + r.land_vec[1] + r.land_vec[2] + r.land_vec[3]
+        spread = net.plane_swap(w, lambda p: r.vec_z, lambda p: r.vec_all.at[p])
+        qkv()
+        r.qkv_z[...] = sum(r.land_qkv[k].astype(F32) for k in range(4)).astype(BF16).reshape(8, 32, 384)
+        last = net.plane_swap(w, lambda p: r.qkv_z.at[p], lambda p: r.g_qkv.at[p])
+        out()
+        r.g_out[...] = sum(r.land_out[k].astype(F32) for k in range(4))
+        spread()
+        r.vec_sum[...] = sum(r.vec_all[p] for p in range(8))
+        for p in range(8):
+            r.vec_part[p] = r.vec_all[p, 16:24]
+        inner()
+        last()
+        grad()
+
+    return run(
+        body,
+        dict(
+            grad_low=(grad_low, ANY),
+            qkv=(g_qkv, ANY),
+            out=(g_out, ANY),
+            inner=(red_in, ANY),
+            vecs=(vecs, VMEM),
+        ),
+        dict(
+            grad=((128, width), BF16, ANY),
+            g_qkv=((8, 32, 384), BF16, ANY),
+            g_in=((8, 32, ff), BF16, ANY),
+            g_out=((32, width), F32, VMEM),
+            vec_sum=((24, width), F32, VMEM),
+            vec_part=((8, 8, width), F32, VMEM),
+        ),
+        dict(
+            land_qkv=VMEM((4, 4, 64, 384), BF16),
+            land_out=VMEM((4, 32, width), BF16),
+            land_vec=VMEM((4, 24, width), F32),
+            vec_z=VMEM((24, width), F32),
+            vec_all=VMEM((8, 24, width), F32),
+            qkv_z=VMEM((8, 32, 384), BF16),
+        ),
+        number,
+    )
+
+
+def plane_body(
+    hidden_in,
+    document_index,
+    out_grad,
+    qkv_weight,
+    value_bias,
+    attention_output_weight,
+    ffn_in_weight,
+    ffn_out_weight,
+    biases,
+    norm_gains,
+):
+    layers = qkv_weight.shape[0]
+    width = hidden_in.shape[1]
+    inner = ffn_in_weight.shape[2]
+    share = inner // 8
+    d, t = lax.axis_index(DP), lax.axis_index(CTX)
+    y = lax.rem(t, 2)
+    part = d * 2 + y
+    packed = jnp.concatenate([biases, norm_gains, value_bias], axis=1).reshape(-1)
+    per_owner = packed.shape[0] // layers
+    n_bias, n_gain = biases.shape[1], norm_gains.shape[1]
+    sent = types.SimpleNamespace(
+        hidden=hidden_in,
+        docs=jnp.broadcast_to(document_index, (8, 128)),
+        vec=jnp.pad(packed, (0, 2048 - packed.shape[0])).reshape(16, 128),
+        qkv=qkv_weight.reshape(layers, 32, 3, 8, width // 8)
+        .transpose(0, 3, 1, 2, 4)
+        .reshape(layers, 8, 32, 3 * width // 8),
+        inner=ffn_in_weight.reshape(layers, 32, 4, 4, 2, share // 4)
+        .transpose(0, 2, 4, 1, 3, 5)
+        .reshape(layers, 8, 32, share),
+        out=attention_output_weight[0],
+    )
+    got = start_kernel(sent, 0)
+    docs = got.docs_all[:, 0].reshape(2, 2, 2, 128).transpose(0, 2, 1, 3).reshape(1024)
+    docs = (jnp.broadcast_to(docs[None], (8, 1024)), jnp.broadcast_to(docs[:, None], (1024, 128)))
+    vec = (
+        got.vec_all.reshape(4, 2, 4, 2048)
+        .transpose(0, 2, 1, 3)
+        .reshape(32, 2048)[:, : layers * per_owner]
+        .astype(F32)
+    )
+    owned = vec.reshape(32, layers, per_owner)
+    bias = owned[:, :, :n_bias].transpose(1, 0, 2).reshape(layers, -1)
+    gain = owned[:, :, n_bias : n_bias + n_gain].transpose(1, 0, 2).reshape(layers, -1)
+    v_bias = owned[:, :, n_bias + n_gain :].transpose(1, 0, 2).reshape(layers, -1)
+    vecs, tpbs = [], []
+    for layer in range(layers):
+        row = bias[layer]
+        after = 2 * width + inner
+        vecs.append(
+            jnp.stack(
+                [
+                    gain[layer, :width],
+                    row[after + width : after + 2 * width],
+                    row[width : 2 * width],
+                    gain[layer, width:],
+                    row[after + 2 * width : after + 3 * width],
+                    row[after : after + width],
+                    jnp.zeros((width,), F32),
+                    jnp.zeros((width,), F32),
+                ]
+            )
+        )
+        head = lax.dynamic_slice_in_dim(row, part * 128, 128)
+        head_v = lax.dynamic_slice_in_dim(v_bias[layer], part * 128, 128)
+        units = lax.dynamic_index_in_dim(
+            row[2 * width : after].reshape(4, 4, 2, share // 4).transpose(0, 2, 1, 3).reshape(8, share),
+            part,
+            0,
+            keepdims=False,
+        )
+        first = jnp.concatenate([head, jnp.zeros((128,), F32), head_v, jnp.zeros((width - 384,), F32)])
+        tpbs.append(
+            jnp.concatenate(
+                [first[None], jnp.pad(units, (0, width - share))[None], jnp.zeros((6, width), F32)]
+            )
+        )
+    state, low = None, got.hidden_row
+    w_qkv, out_z = got.qkv_all.reshape(width, 384), got.out_all
+    kept, number = [], 1
+    for layer in range(layers):
+        bring = bringing(
+            inner=got.inner_z[layer].reshape(4, 64, share),
+            ffo=ffn_out_weight[layer],
+        )
+        att = attend_kernel(state, low, w_qkv, out_z, docs, vecs[layer], tpbs[layer], bring, number)
+        w_in, w_ffo = att.inner_all.reshape(width, share), att.ffo_all.reshape(share, width)
+        if layer + 1 < layers:
+            bring = bringing(
+                qkv=got.qkv_one.reshape(4, 64, 384),
+                out=attention_output_weight[layer + 1],
+            )
+        else:
+            bring = bringing(swap=out_grad)
+        feed = feed_kernel(
+            att.normed, att.normed_low, w_in, w_ffo, vecs[layer], tpbs[layer], bring, number + 1
+        )
+        number += 2
+        kept.append((att, feed, w_qkv, w_in, w_ffo))
+        state, low = feed.state, feed.state_low
+        if layer + 1 < layers:
+            w_qkv, out_z = feed.qkv_all.reshape(width, 384), feed.out_all
+    grad = feed.swapped
+    qkv_done, in_done = [None] * layers, [None] * layers
+    out_done, ffo_done = [None] * layers, [None] * layers
+    sums = []
+    bring = bringing(swap=low)
+    red_qkv = None
+    for layer in reversed(range(layers)):
+        att, feed, w_qkv, w_in, w_ffo = kept[layer]
+        back = feed_back_kernel(grad, feed, att.hat, att.root, w_in, w_ffo, vecs[layer], bring, number)
+        if layer + 1 == layers:
+            out = back.swapped
+        else:
+            out_done[layer + 1] = back.red_out
+            in_done[layer + 1] = back.plane_all
+            red_qkv = back.red_qkv
+        bring = bringing(
+            ffo=back.g_ffo.reshape(4, 128, width),
+            inner=back.g_in.reshape(4, 4, 64, share),
+        )
+        if red_qkv is not None:
+            bring.plane = red_qkv.reshape(8, 32, 384)
+        turn = attend_back_kernel(back.back_one, back.branch, att, w_qkv, docs, bring, number + 1)
+        number += 2
+        if red_qkv is not None:
+            qkv_done[layer + 1] = turn.plane_all
+        ffo_done[layer] = turn.red_ffo
+        sums.append((back.sums, turn.sums))
+        grad = turn.grad
+        red_in = turn.red_in.reshape(8, 32, share)
+        bring = bringing(qkv=turn.g_qkv.reshape(4, 4, 64, 384), out=turn.g_out_z, plane=red_in)
+    packed = [back.at[6, 0:128].set(turn[0, 0:128]).at[6, 128:256].set(turn[0, 256:384]) for back, turn in sums]
+    packed = jnp.concatenate(
+        [packed[1][0:6], jnp.zeros((2, width), F32), packed[0][0:6], jnp.zeros((2, width), F32)]
+        + [packed[1][6:7], packed[0][6:7], jnp.zeros((6, width), F32)]
+    )
+    end = end_kernel(
+        grad.astype(BF16), turn.g_qkv.reshape(4, 4, 64, 384), turn.g_out_z, red_in, packed, number
+    )
+    out_done[0], in_done[0], qkv_done[0] = end.g_out, end.g_in, end.g_qkv
+    index = d * 8 + t
+    bias_all, gain_all, value_all = [], [], []
+    for layer in range(layers):
+        rows = end.vec_sum[8 * layer : 8 * layer + 8]
+        parts = end.vec_part[:, layer]
+        bias_all.append(
+            jnp.concatenate(
+                [
+                    parts[:, 0:128].reshape(-1),
+                    rows[BO],
+                    parts[:, 256 : 256 + share].reshape(4, 2, 4, share // 4).transpose(0, 2, 1, 3).reshape(-1),
+                    rows[B2],
+                    rows[S1],
+                    rows[S2],
+                ]
+            )
+        )
+        gain_all.append(jnp.concatenate([rows[G1], rows[G2]]))
+        value_all.append(parts[:, 128:256].reshape(-1))
+
+    def own(items, size):
+        return lax.dynamic_slice_in_dim(jnp.stack(items), index * size, size, 1)
+
+    return (
+        out,
+        end.grad.astype(F32),
+        jnp.stack(
+            [
+                item.reshape(8, 32, 3, 128).transpose(1, 2, 0, 3).reshape(32, 3 * width).astype(F32)
+                for item in qkv_done
+            ]
+        ),
+        own(value_all, width // 32),
+        jnp.stack(out_done),
+        jnp.stack(
+            [
+                item.reshape(4, 2, 32, 4, share // 4).transpose(2, 0, 3, 1, 4).reshape(32, inner).astype(F32)
+                for item in in_done
+            ]
+        ),
+        jnp.stack(ffo_done),
+        own(bias_all, n_bias),
+        own(gain_all, n_gain),
+    )
+
+
+def fits_plane(mesh):
+    return mesh.shape[DP] == 4 and mesh.shape[CTX] == 8
+
+
 def solution(mesh):
     return jax.shard_map(
-        body,
+        plane_body if fits_plane(mesh) else body,
         mesh=mesh,
         in_specs=(
-            P(("dp", "ctx"), None),
-            P("dp", "ctx"),
-            P(("dp", "ctx"), None),
-            P(None, ("dp", "ctx"), None),
-            P(None, ("dp", "ctx")),
-            P(None, ("dp", "ctx"), None),
-            P(None, ("dp", "ctx"), None),
-            P(None, ("dp", "ctx"), None),
-            P(None, ("dp", "ctx")),
-            P(None, ("dp", "ctx")),
+            P(BOTH, None),
+            P(DP, CTX),
+            P(BOTH, None),
+            P(None, BOTH, None),
+            P(None, BOTH),
+            P(None, BOTH, None),
+            P(None, BOTH, None),
+            P(None, BOTH, None),
+            P(None, BOTH),
+            P(None, BOTH),
         ),
         out_specs=(
-            P(("dp", "ctx"), None),
-            P(("dp", "ctx"), None),
-            P(None, ("dp", "ctx"), None),
-            P(None, ("dp", "ctx")),
-            P(None, ("dp", "ctx"), None),
-            P(None, ("dp", "ctx"), None),
-            P(None, ("dp", "ctx"), None),
-            P(None, ("dp", "ctx")),
-            P(None, ("dp", "ctx")),
+            P(BOTH, None),
+            P(BOTH, None),
+            P(None, BOTH, None),
+            P(None, BOTH),
+            P(None, BOTH, None),
+            P(None, BOTH, None),
+            P(None, BOTH, None),
+            P(None, BOTH),
+            P(None, BOTH),
         ),
         check_vma=False,
     )

time: 3450 us -> 517 us (0.15)
  waiting for transfers between devices: 2930 us -> 0 us
  Pallas kernels: 0 us -> 472 us
  matrix products: 185 us -> 0 us
  local copies, waits for them, and re-layouts: 163 us -> 24.6 us
  other arithmetic: 80.6 us -> 9.06 us
  blocking collectives: 62.1 us -> 0 us
    reduce_scatter x6 -> x0, waiting for transfers between devices: 1720 us -> none  [the longest x2 717 us: body(): lax.psum_scatter(grad_second, ('dp', 'ctx'), scatter_dimension=0, tiled=T...]
    unnamed x32 -> x0, waiting for transfers between devices: 619 us -> none
    all_gather x12 -> x0, waiting for transfers between devices: 592 us -> none  [the longest x2 155 us: body(): lax.all_gather(ffn_in_weight[layer], ('dp', 'ctx'), axis=0, tiled=True)]
    pallas_call x0 -> x10, Pallas kernels: none -> 472 us  [run(): pl.pallas_call(kernel, out_shape=[jax.ShapeDtypeStruct(shape, dtype) for...]
    dot_general x167 -> x0, matrix products: 179 us -> none  [the longest x7 46.2 us: cross(): lax.dot_general(left, right_operand, (((0,), (0,)), ((), ())), preferred_...]
    dynamic_slice x112 -> x5, local copies, waits for them, and re-layouts: 73.3 us -> 0.33 us  [the longest x2 0.16 us: plane_body(): head = lax.dynamic_slice_in_dim(row, part * 128, 128)]
    unnamed x187 -> x56, local copies, waits for them, and re-layouts: 68.8 us -> 0.91 us
    unnamed x1 -> x0, blocking collectives: 43 us -> none
  transfers between devices with their start and end apart: 25 -> 0, of which waited for: 25 -> 0; matrix products, arithmetic and copies ran while one was open for 6% -> 0% of each run, Pallas kernels for 0% -> 0%
where the time goes in v1:
time: 517 us; the launch traced here: 508 us
  Pallas kernels  472 us (91%)
  local copies, waits for them, and re-layouts  24.6 us (5%)
  other arithmetic  9.06 us (2%)
    pallas_call x10, Pallas kernels, run(): pl.pallas_call(kernel, out_shape=[jax.ShapeDtypeStruct(shape, dtype) for...  472 us

profile of v1, /device:TPU:0, one launch (start us, length us, event | category | flops | bytes accessed | tf_op | source)
XLA Modules:
  0.0 507.6 jit_solution(6527658449021373797)
XLA Ops:
  0.7 1.6 slice_bitcast_fusion.3
  2.2 1.4 reshape.311
  3.6 0.2 copy.63
  3.9 1.0 reshape.312.refs_4_
  5.0 0.2 copy.64
  5.2 1.1 reshape.310.refs_3_
  6.4 0.6 pad_bitcast_fusion.refs_2_
  7.0 0.6 broadcast_in_dim.32.refs_1_
  7.6 45.4 %shard_map.169 = (bf16[128,1024]{1,0:T(8,128)(2,1)}, s32[8,8,128]{2,1,0:T(8,128)}, bf16[8,4,16,128]{3,2,1,0:T(8,128)(2,1)}, bf16[8,32,384]{2,1,0:T(8,128)(2,1)},...) custom-call(bf16[128,1024]{1,0:T(8,128)(2,1)} %refs_0_.1, ...), custom_call_target="tpu_custom_call" | custom-call | bytes 8388608 | tf_op jit(solution)/shard_map/pallas_call | solution.py:677
  53.0 1.0 reshape.314
  54.0 0.1 copy.65
  54.3 0.3 slice_reduce_fusion
  54.6 0.1 squeeze.78
  54.7 0.1 squeeze.83
  54.9 0.1 slice_bitcast_fusion.5
  55.0 0.1 slice_reduce_fusion.2
  55.4 0.1 slice.294
  55.6 0.1 slice.281
  55.8 0.7 pad_maximum_fusion.2
  56.4 0.1 slice_bitcast_fusion.6
  56.6 0.1 reshape.318
  56.7 0.7 stack.89.refs_5_.refs_4_.refs_10_
  57.3 0.8 slice.268
  58.1 1.0 broadcast_in_dim.35.refs_4_.refs_9_
  59.1 0.6 broadcast_in_dim.34.refs_3_.refs_8_
  59.7 0.8 fusion.5
  60.6 0.8 slice_bitcast_fusion
  61.4 54.6 %shard_map.170 = (bf16[1024,1024]{1,0:T(8,128)(2,1)}, bf16[1024,384]{1,0:T(8,128)(2,1)}, bf16[1024,128]{1,0:T(8,128)(2,1)}, f32[1024,128]{1,0:T(8,128)}, bf16[2,...) custom-call(bf16[128,1024]{1,0:T(8,128)(2,1)} %get-tuple-element.135, ...), custom_call_target="tpu_custom_call" | custom-call | bytes 8388608 | tf_op jit(solution)/shard_map/pallas_call | solution.py:677
  116.0 34.8 %shard_map.171 = (bf16[1024,1024]{1,0:T(8,128)(2,1)}, bf16[1024,512]{1,0:T(8,128)(2,1)}, f32[1024,512]{1,0:T(8,128)}, f32[128,1024]{1,0:T(8,128)}, bf16[128,1024...) custom-call(f32[128,1024]{1,0:T(8,128)} %get-tuple-element.141.refs_, ...), custom_call_target="tpu_custom_call" | custom-call | bytes 8388608 | tf_op jit(solution)/shard_map/pallas_call | solution.py:677
  150.8 0.7 stack.94.refs_5_.refs_4_.refs_10_
  151.5 50.5 %shard_map.172 = (bf16[1024,1024]{1,0:T(8,128)(2,1)}, bf16[1024,384]{1,0:T(8,128)(2,1)}, bf16[1024,128]{1,0:T(8,128)(2,1)}, f32[1024,128]{1,0:T(8,128)}, bf16[2,...) custom-call(bf16[128,1024]{1,0:T(8,128)(2,1)} %get-tuple-element.146, ...), custom_call_target="tpu_custom_call" | custom-call | bytes 8388608 | tf_op jit(solution)/shard_map/pallas_call | solution.py:677
  202.0 40.9 %shard_map.173 = (bf16[1024,1024]{1,0:T(8,128)(2,1)}, bf16[1024,512]{1,0:T(8,128)(2,1)}, f32[1024,512]{1,0:T(8,128)}, f32[128,1024]{1,0:T(8,128)}, bf16[128,1024...) custom-call(f32[128,1024]{1,0:T(8,128)} %get-tuple-element.150.refs_0_, ...), custom_call_target="tpu_custom_call" | custom-call | bytes 8388608 | tf_op jit(solution)/shard_map/pallas_call | solution.py:677
  242.9 43.6 %shard_map.174 = (bf16[512,1024]{1,0:T(8,128)(2,1)}, bf16[1024,512]{1,0:T(8,128)(2,1)}, f32[128,1024]{1,0:T(8,128)}, bf16[128,1024]{1,0:T(8,128)(2,1)}, f32[8,1024]{1,0:T(8,128)}, /*index=5*/bf16[128,1024]{1,0:T(8,128)(2,1)}) custom-call(bf16[128,1024]{1,0:T(8,128)(2,1)} %get-tuple-element.154.refs_0_, f32[128,1024]{1,0:T(8,128)} %get-tuple-element.155.refs_1_, ...), custom_call_target="tpu_custom_call" | custom-call | bytes 8388608 | tf_op jit(solution)/shard_map/pallas_call | solution.py:677
  286.5 52.3 %shard_map.175 = (f32[128,1024]{1,0:T(8,128)}, bf16[1024,384]{1,0:T(8,128)(2,1)}, bf16[4,32,1024]{2,1,0:T(8,128)(2,1)}, f32[8,384]{1,0:T(8,128)}, f32[128,1024]{1,0:T(8,128)}, /*index=5*/bf16[4,64,512]{2,1,0:T(8,128)(2,1)}) custom-call(f32[128,1024]{1,0:T(8,128)} %get-tuple-element.164.refs_0_, bf16[128,1024]{1,0:T(8,128)(2,1)} %get-tuple-element.165.refs_1_, ...), custom_call_target="tpu_custom_call" | custom-call | bytes 8388608 | tf_op jit(solution)/shard_map/pallas_call | solution.py:677
  338.8 0.7 fusion.11
  339.5 0.1 scatter.16
  339.6 0.4 scatter.19
  340.1 40.1 %shard_map.176 = (bf16[512,1024]{1,0:T(8,128)(2,1)}, bf16[1024,512]{1,0:T(8,128)(2,1)}, f32[128,1024]{1,0:T(8,128)}, bf16[128,1024]{1,0:T(8,128)(2,1)}, f32[8,10...) custom-call(f32[128,1024]{1,0:T(8,128)} %get-tuple-element.173.refs_0_, ...), custom_call_target="tpu_custom_call" | custom-call | bytes 8388608 | tf_op jit(solution)/shard_map/pallas_call | solution.py:677
  380.2 50.1 %shard_map.177 = (f32[128,1024]{1,0:T(8,128)}, bf16[1024,384]{1,0:T(8,128)(2,1)}, bf16[4,32,1024]{2,1,0:T(8,128)(2,1)}, f32[8,384]{1,0:T(8,128)}, f32[128,1024]{...) custom-call(f32[128,1024]{1,0:T(8,128)} %get-tuple-element.184.refs_0_, ...), custom_call_target="tpu_custom_call" | custom-call | bytes 8388608 | tf_op jit(solution)/shard_map/pallas_call | solution.py:677
  430.3 0.8 fusion.12
  431.1 0.1 scatter.14
  431.3 0.2 scatter.15
  431.5 1.9 concatenate.43.refs_4_
  433.4 1.8 convert_element_type.80.refs_0_
  435.2 59.7 %shard_map.178 = (bf16[128,1024]{1,0:T(8,128)(2,1)}, bf16[8,32,384]{2,1,0:T(8,128)(2,1)}, bf16[8,32,512]{2,1,0:T(8,128)(2,1)}, f32[32,1024]{1,0:T(8,128)}, f32[24,1024]{1,0:T(8,128)}, /*index=5*/f32[8,8,1024]{2,1,0:T(8,128)}) custom-call(bf16[128,1024]{1,0:T(8,128)(2,1)} %convert_element_type.80.refs_0_, bf16[4,4,64,384]{3,2,1,0:T(8,128)(2,1)} %bitcast.158, ...), custom_call_target="tpu_custom_call" | custom-call | bytes 8388608 | tf_op jit(solution)/shard_map/pallas_call | solution.py:677
  494.9 1.3 fusion.7
  496.3 0.6 fusion.4
  496.9 1.1 fusion.6
  498.3 0.7 fusion.2
  499.0 1.0 pad_maximum_fusion
  500.1 0.4 copy.45
  500.5 0.2 convert_element_type.90
  500.8 0.4 copy.46
  501.2 0.2 convert_element_type.93
  501.4 1.0 maximum_convert_fusion
  502.4 0.7 pad_maximum_fusion.1
  503.2 0.6 fusion.3
  503.9 0.2 copy.43
  504.1 0.1 convert_element_type.84
  504.3 0.2 copy.44
  504.5 0.1 convert_element_type.87
  504.6 0.9 maximum_convert_fusion.1
  505.6 0.8 convert_element_type.81
  506.4 0.7 copy.85
  (100 shorter events, 1.3 us)
Async XLA Ops:
  0.6 4.3 copy-start.4
  3.9 2.4 copy-start.15
  3.9 2.4 copy-start.17
  3.9 2.4 copy-start.18
  3.9 3.1 copy-start.16
  53.0 6.7 %copy-start.1 = (bf16[2,8,32,512]{3,2,1,0:T(8,128)(2,1)S(1)}, bf16[2,8,32,512]{3,2,1,0:T(8,128)(2,1)}, u32[]{:S(2)}) copy-start(bf16[2,8,32,512]{3,2,1,0:T(8,128)(2,1)} %get-tuple-element.140) | copy-start | bytes 1572868
  54.0 6.6 %copy-start = (bf16[2,128,1024]{2,1,0:T(8,128)(2,1)S(1)}, bf16[2,128,1024]{2,1,0:T(8,128)(2,1)}, u32[]{:S(2)}) copy-start(bf16[2,128,1024]{2,1,0:T(8,128)(2,1)} %param.25) | copy-start | bytes 1572868
  286.5 53.0 %copy-start.14 = (f32[8,1024]{1,0:T(8,128)S(1)}, f32[8,1024]{1,0:T(8,128)}, u32[]{:S(2)}) copy-start(f32[8,1024]{1,0:T(8,128)} %get-tuple-element.200) | copy-start | bytes 98308
  380.2 50.9 %copy-start.13 = (f32[8,1024]{1,0:T(8,128)S(1)}, f32[8,1024]{1,0:T(8,128)}, u32[]{:S(2)}) copy-start(f32[8,1024]{1,0:T(8,128)} %get-tuple-element.198) | copy-start | bytes 98308
  430.3 68.6 %copy-start.2 = (f32[128,1024]{1,0:T(8,128)S(1)}, f32[128,1024]{1,0:T(8,128)}, u32[]{:S(2)}) copy-start(f32[128,1024]{1,0:T(8,128)} %get-tuple-element.211) | copy-start | bytes 1572868
  430.3 68.6 %copy-start.3 = (f32[128,1024]{1,0:T(8,128)S(1)}, f32[128,1024]{1,0:T(8,128)}, u32[]{:S(2)}) copy-start(f32[128,1024]{1,0:T(8,128)} %get-tuple-element.210) | copy-start | bytes 1572868
  494.9 5.1 %copy-start.8 = (bf16[8,32,512]{2,1,0:T(8,128)(2,1)S(1)}, bf16[8,32,512]{2,1,0:T(8,128)(2,1)}, u32[]{:S(2)}) copy-start(bf16[8,32,512]{2,1,0:T(8,128)(2,1)} %get-tuple-element.208) | copy-start | bytes 786436
  498.1 2.6 copy-start.7
  500.1 2.4 copy-start.11
  500.1 2.4 copy-start.12
  500.5 3.3 copy-start.10
  501.2 3.0 copy-start.9
  502.4 3.1 copy-start.5
  503.9 2.5 copy-start.6
